TPU v7x, 32 devices: a whole 2x2x4 slice. The times are simulated.
32 devices in a mesh: expert: 4 (over y, x), dp: 4 (over z), mp: 2 (over core).
Axes of the slice: x: 2, y: 2, z: 4, core: 2. Of those that a mesh axis runs over, the one named last changes fastest.
Arguments:
- tokens: bfloat16 [6304, 768], P(('expert', 'dp', 'mp')), may hold values from -6 to 6
- cotangent: bfloat16 [6304, 768], P(('expert', 'dp', 'mp')), may hold values from -6 to 6
- routes: int32 [6304, 2], P(('expert', 'dp', 'mp')), may hold values from 0 to 3, all different within a row
- norm1_gain: float32 [768], replicated, may hold values from 0.5 to 1.5
- norm1_shift: float32 [768], replicated, may hold values from -1 to 1
- attn_input: bfloat16 [768, 3, 768], P('dp', None, 'mp'), may hold values from -0.21875 to 0.21875
- input_bias: float32 [2, 768], replicated, may hold values from -1 to 1
- attn_output: bfloat16 [768, 768], P('dp', 'mp'), may hold values from -0.875 to 0.875
- output_bias: float32 [768], replicated, may hold values from -1 to 1
- norm2_gain: float32 [768], replicated, may hold values from 0.5 to 1.5
- norm2_shift: float32 [768], replicated, may hold values from -1 to 1
- router_weight: bfloat16 [768, 4], replicated, may hold values from -0.15625 to 0.15625
- up_weight: bfloat16 [4, 768, 3072], P('expert', None, ('dp', 'mp')), may hold values from -0.21875 to 0.21875
- up_bias: bfloat16 [4, 3072], P('expert', ('dp', 'mp')), may hold values from -0.8984375 to 0.8984375
- down_weight: bfloat16 [4, 3072, 768], P('expert', ('dp', 'mp')), may hold values from -0.4375 to 0.4375
- down_bias: bfloat16 [4, 768], P('expert', ('dp', 'mp')), may hold values from -6 to 6
Outputs:
- mixed: bfloat16 [6304, 768], P(('expert', 'dp', 'mp'))
- tokens_grad: float32 [6304, 768], P(('expert', 'dp', 'mp'))
- norm1_gain_grad: float32 [768], replicated
- norm1_shift_grad: float32 [768], replicated
- attn_input_grad: float32 [768, 3, 768], P('dp', None, 'mp')
- input_bias_grad: float32 [2, 768], replicated
- attn_output_grad: float32 [768, 768], P('dp', 'mp')
- output_bias_grad: float32 [768], replicated
- norm2_gain_grad: float32 [768], replicated
- norm2_shift_grad: float32 [768], replicated
- router_grad: float32 [768, 4], replicated
- up_weight_grad: float32 [4, 768, 3072], P('expert', None, ('dp', 'mp'))
- up_bias_grad: float32 [4, 3072], P('expert', ('dp', 'mp'))
- down_weight_grad: float32 [4, 3072, 768], P('expert', ('dp', 'mp'))
- down_bias_grad: float32 [4, 768], P('expert', ('dp', 'mp'))
Inputs may be any that keep to these rules, and one draw needn't show every extreme that they name: `routes`: each row names two different experts.
All inputs are finite; a program needn't handle non-finite values.
Results may differ from a plain program's by a relative error of at most 0.017.
Values may be sent and summed in bfloat16 or wider, within the bound.
A program may use at most 128 MiB of HBM per device.

v0:
```python
import jax
import jax.numpy as jnp
from jax import lax
from jax.sharding import PartitionSpec as P

HEAD_DIM = 64
EPSILON = 1e-06
BF = jnp.bfloat16
F32 = jnp.float32


def mm(spec, a, b):
    return jnp.einsum(spec, a, b, preferred_element_type=F32)


def norm_stats(values):
    center = values - jnp.mean(values, axis=-1, keepdims=True)
    inverse = lax.rsqrt(jnp.mean(center * center, axis=-1, keepdims=True) + EPSILON)
    return center * inverse, inverse


def norm_pull(xhat, inverse, gain, upstream):
    u = upstream * gain
    mean_u = jnp.mean(u, axis=-1, keepdims=True)
    mean_ux = jnp.mean(u * xhat, axis=-1, keepdims=True)
    return (u - mean_u - xhat * mean_ux) * inverse


def swap(value):
    return lax.ppermute(value, "mp", [(0, 1), (1, 0)])


def from_axis(shard, count):
    return [shard] + [to_owner(shard, count - k, count) for k in range(1, count)]


def across(value, j, count):
    return lax.ppermute(value, "expert", [(e, e ^ j) for e in range(count)])


def sum_all(value):
    for axis in ("mp", "expert", "dp"):
        count, step = lax.axis_size(axis), 1
        while step < count:
            value = value + lax.ppermute(value, axis, [(i, i ^ step) for i in range(count)])
            step *= 2
    return value


def to_owner(chunk, k, count):
    return lax.ppermute(chunk, "dp", [(z, (z + k) % count) for z in range(count)])


def attend(project, bias, heads):
    images, seq = project.shape[0], project.shape[1]
    shape = (images, seq, heads, HEAD_DIM)
    width = heads * HEAD_DIM
    q = (project[:, :, :width] + bias[0]).astype(BF).reshape(shape)
    k = project[:, :, width : 2 * width].astype(BF).reshape(shape)
    v = (project[:, :, 2 * width :] + bias[1]).astype(BF).reshape(shape)
    scores = mm("iqhe,ikhe->ihqk", q, k) * HEAD_DIM ** (-0.5)
    probs = jax.nn.softmax(scores, axis=-1)
    mixed = mm("ihqk,ikhe->iqhe", probs.astype(BF), v).astype(BF)
    return (q, k, v, probs), mixed.reshape(images, seq, width)


def attend_back(kept, grad_mixed):
    q, k, v, probs = kept
    grad_mixed = grad_mixed.reshape(q.shape)
    scale = HEAD_DIM ** (-0.5)
    grad_v = mm("ihqk,iqhe->ikhe", probs.astype(BF), grad_mixed)
    grad_probs = mm("iqhe,ikhe->ihqk", grad_mixed, v)
    grad_scores = (
        probs * (grad_probs - jnp.sum(probs * grad_probs, axis=-1, keepdims=True))
    ).astype(BF)
    grad_q = mm("ihqk,ikhe->iqhe", grad_scores, k) * scale
    grad_k = mm("ihqk,iqhe->ikhe", grad_scores, q) * scale
    images, seq = q.shape[:2]
    return jnp.concatenate(
        [g.astype(BF).reshape(images, seq, -1) for g in (grad_q, grad_k, grad_v)], axis=-1
    )


def on_device(
    tokens, cotangent, routes, norm1_gain, norm1_shift, attn_input, input_bias, attn_output,
    output_bias, norm2_gain, norm2_shift, router_weight, up_weight, up_bias, down_weight, down_bias,
):
    rows, width = tokens.shape
    local = attn_input.shape[2]
    heads = local // HEAD_DIM
    mp_index, dp_index = lax.axis_index("mp"), lax.axis_index("dp")
    expert_index = lax.axis_index("expert")
    mp_count, dp_count = lax.axis_size("mp"), lax.axis_size("dp")
    expert_axis = lax.axis_size("expert")
    experts = router_weight.shape[1]
    capacity = 2 * rows // experts
    padded = -(-capacity // 8) * 8
    slots = experts * padded

    shard = jnp.concatenate(
        [attn_input.reshape(attn_input.shape[0], 3 * local), attn_output], axis=1
    )
    part = shard.shape[0] // expert_axis
    mine = lax.dynamic_slice_in_dim(shard, expert_index * part, part, 0)
    column = jnp.stack(from_axis(mine, dp_count))
    column, up_own, down_own = lax.optimization_barrier((column, up_weight[0], down_weight[0]))
    column = lax.dynamic_slice_in_dim(
        jnp.concatenate([column, column]), lax.rem(dp_count - dp_index, dp_count), dp_count, 0
    )
    attn_full = jnp.zeros((dp_count, expert_axis) + mine.shape, BF)
    for j in range(expert_axis):
        piece = across(column, j, expert_axis) if j else column
        attn_full = lax.dynamic_update_slice(
            attn_full, piece[:, None], (0, expert_index ^ j, 0, 0)
        )
    attn_full = attn_full.reshape(width, 4 * local)
    input_full, output_full = attn_full[:, : 3 * local], attn_full[:, 3 * local :]

    other_tokens = swap(tokens)
    ff_part = up_weight.shape[2]
    bias_part = down_bias.shape[1]
    ups = from_axis(up_own, dp_count)
    downs = from_axis(down_own, dp_count)
    bias_own = jnp.concatenate([up_bias, down_bias], axis=1)
    biases = from_axis(bias_own, dp_count)

    flat_routes = jnp.concatenate([routes[:, 0], routes[:, 1]])
    expert_ids = jnp.arange(experts, dtype=jnp.int32)
    one_hot = flat_routes[:, None] == expert_ids[None, :]
    order = jnp.arange(2 * rows, dtype=jnp.int32)
    before = (order[:, None] > order[None, :]).astype(BF)
    earlier = mm("ab,be->ae", before, one_hot.astype(BF))
    position = jnp.sum(jnp.where(one_hot, earlier, 0.0), axis=1).astype(jnp.int32)
    target = jnp.where(position < capacity, flat_routes * padded + position, slots)
    place = (target[:, None] == jnp.arange(slots, dtype=jnp.int32)[None, :]).astype(BF)
    place_both = place[:rows] + place[rows:]

    pair = jnp.stack([tokens, other_tokens]).astype(F32)
    xhat1, inverse1 = norm_stats(pair)
    normed = (xhat1 * norm1_gain + norm1_shift).astype(BF)
    local_bias = lax.dynamic_slice_in_dim(input_bias, mp_index * local, local, 1)
    project = mm("itd,df->itf", normed, input_full)
    kept, mixed_heads = attend(project, local_bias, heads)
    from_other = swap(mm("tf,df->td", mixed_heads[1], output_full))
    residual = (
        tokens.astype(F32) + mm("tf,df->td", mixed_heads[0], output_full) + from_other + output_bias
    )

    xhat2, inverse2 = norm_stats(residual)
    routed = (xhat2 * norm2_gain + norm2_shift).astype(BF)
    gates_all = jax.nn.softmax(mm("td,de->te", routed, router_weight), axis=-1)
    pick_first, pick_second = one_hot[:rows], one_hot[rows:]
    gate_first = jnp.sum(jnp.where(pick_first, gates_all, 0.0), axis=-1, keepdims=True)
    gate_second = jnp.sum(jnp.where(pick_second, gates_all, 0.0), axis=-1, keepdims=True)
    upstream = cotangent.astype(F32)
    route_grads = jnp.concatenate([gate_first * upstream, gate_second * upstream]).astype(BF)
    send = jnp.concatenate(
        [
            mm("ts,td->sd", place_both, routed).astype(BF),
            mm("ts,td->sd", place, route_grads).astype(BF),
        ],
        axis=1,
    ).reshape(experts, padded, 2 * width)
    received = lax.all_to_all(send, "expert", split_axis=0, concat_axis=0, tiled=True)
    received = received.reshape(-1, 2 * width)
    count = received.shape[0]
    both = jnp.concatenate([received, swap(received)], axis=0)
    slab, slab_grad = both[:, :width], both[:, width:]

    produced = grad_slab = 0.0
    up_sums, down_sums, bias_sums = [], [], []
    column_sum = jnp.sum(slab_grad, axis=0, dtype=F32).reshape(dp_count, mp_count, bias_part)
    column_sum = lax.dynamic_index_in_dim(column_sum, mp_index, 1, keepdims=False)
    bias_row = jnp.zeros((dp_count, mp_count, bias_part), F32)
    for k in range(dp_count):
        owner = lax.rem(dp_index + k, dp_count)
        bias_k = biases[k].astype(F32)
        bias_row = lax.dynamic_update_slice(
            bias_row, bias_k[:, None, ff_part:], (owner, mp_index, jnp.int32(0))
        )
        pre = mm("td,df->tf", slab, ups[k]) + bias_k[:, :ff_part]
        cdf = 0.5 * (1.0 + lax.erf(pre * (0.5**0.5)))
        slope = cdf + pre * (jnp.exp(-0.5 * pre * pre) * 0.3989422804014327)
        hidden = (pre * cdf).astype(BF)
        produced = produced + mm("tf,fd->td", hidden, downs[k])
        grad_pre = (mm("td,fd->tf", slab_grad, downs[k]) * slope).astype(BF)
        grad_slab = grad_slab + mm("tf,df->td", grad_pre, ups[k])
        down_part = mm("tf,td->fd", hidden, slab_grad)
        up_part = mm("td,tf->df", slab, grad_pre)
        bias_grad = jnp.concatenate(
            [
                jnp.sum(grad_pre, axis=0, dtype=F32)[None, :],
                lax.dynamic_index_in_dim(column_sum, owner, 0),
            ],
            axis=1,
        )
        if k:
            down_part = to_owner(down_part.astype(BF), k, dp_count).astype(F32)
            up_part = to_owner(up_part.astype(BF), k, dp_count).astype(F32)
            bias_grad = to_owner(bias_grad, k, dp_count)
        down_sums.append(down_part)
        up_sums.append(up_part)
        bias_sums.append(bias_grad)
    produced = produced + bias_row.reshape(1, -1)
    partial = jnp.concatenate([produced, grad_slab], axis=1)
    back = (partial[:count] + swap(partial[count:].astype(BF)).astype(F32)).astype(BF)
    returned = lax.all_to_all(
        back.reshape(expert_axis, -1, 2 * width), "expert", split_axis=0, concat_axis=0, tiled=True
    ).reshape(slots, 2 * width)

    pick_one = mm("ts,sd->td", place[:rows], returned[:, :width])
    pick_two = mm("ts,sd->td", place[rows:], returned[:, :width])
    result = (residual + gate_first * pick_one + gate_second * pick_two).astype(BF)
    grad_first = jnp.sum(upstream * pick_one, axis=-1, keepdims=True)
    grad_second = jnp.sum(upstream * pick_two, axis=-1, keepdims=True)
    grad_gates = jnp.where(pick_first, grad_first, 0.0) + jnp.where(pick_second, grad_second, 0.0)
    grad_logits = gates_all * (grad_gates - jnp.sum(grad_gates * gates_all, axis=-1, keepdims=True))
    high = lax.Precision.HIGHEST
    router_grad = jnp.dot(routed.astype(F32).T, grad_logits, precision=high)
    grad_routed = jnp.dot(grad_logits, router_weight.astype(F32).T, precision=high)
    grad_routed = grad_routed + mm("ts,sd->td", place_both, returned[:, width:])
    grad_residual = upstream + norm_pull(xhat2, inverse2, norm2_gain, grad_routed)

    grad_branch = grad_residual.astype(BF)
    pair_grad = jnp.stack([grad_branch, swap(grad_branch)])
    grad_mixed = mm("itd,df->itf", pair_grad, output_full).astype(BF)
    output_grad = mm("itd,itf->df", pair_grad, mixed_heads)
    grad_project = attend_back(kept, grad_mixed)
    from_other = swap(mm("tf,df->td", grad_project[1], input_full).astype(BF))
    input_grad = mm("itd,itf->df", normed, grad_project)
    grad_normed = mm("tf,df->td", grad_project[0], input_full) + from_other.astype(F32)
    xhat_own, inverse_own = xhat1[0], inverse1[0]
    tokens_grad = grad_residual + norm_pull(xhat_own, inverse_own, norm1_gain, grad_normed)

    attn_grad = jnp.concatenate([input_grad, output_grad], axis=1).astype(BF)
    attn_grad = attn_grad.reshape(dp_count, expert_axis, part, 4 * local)
    quarter = 0.0
    for j in range(expert_axis):
        piece = lax.dynamic_index_in_dim(attn_grad, expert_index ^ j, 1, keepdims=False)
        quarter = quarter + (across(piece, j, expert_axis) if j else piece).astype(F32)
    quarter = quarter.astype(BF)
    share = 0.0
    for k in range(dp_count):
        piece = lax.dynamic_index_in_dim(
            quarter, lax.rem(dp_index + k, dp_count), 0, keepdims=False
        )
        share = share + (to_owner(piece, k, dp_count) if k else piece).astype(F32)
    share = share.astype(BF)
    attn_grad = jnp.zeros((expert_axis,) + share.shape, F32)
    for j in range(expert_axis):
        piece = (across(share, j, expert_axis) if j else share).astype(F32)
        attn_grad = lax.dynamic_update_slice(attn_grad, piece[None], (expert_index ^ j, 0, 0))
    attn_grad = attn_grad.reshape(-1, 4 * local)

    bias_local = jnp.sum(grad_project, axis=(0, 1), dtype=F32)
    bias_local = jnp.stack([bias_local[:local], bias_local[2 * local :]])
    bias_full = lax.dynamic_update_slice_in_dim(
        jnp.zeros((2, width), F32), bias_local, mp_index * local, 1
    )
    small = jnp.concatenate(
        [
            jnp.sum(grad_normed * xhat_own, axis=0)[None],
            jnp.sum(grad_normed, axis=0)[None],
            bias_full,
            jnp.sum(grad_residual, axis=0)[None],
            jnp.sum(grad_routed * xhat2, axis=0)[None],
            jnp.sum(grad_routed, axis=0)[None],
            router_grad.T,
        ]
    )
    small = sum_all(small)
    bias_total = sum(bias_sums)
    return (
        result,
        tokens_grad,
        small[0],
        small[1],
        attn_grad[:, : 3 * local].reshape(-1, 3, local),
        small[2:4],
        attn_grad[:, 3 * local :],
        small[4],
        small[5],
        small[6],
        small[7:].T,
        sum(up_sums)[None],
        bias_total[:, :ff_part],
        sum(down_sums)[None],
        bias_total[:, ff_part:],
    )


def solution(mesh):
    token_spec = P(("expert", "dp", "mp"), None)
    return jax.shard_map(
        on_device,
        mesh=mesh,
        in_specs=(
            token_spec, token_spec, token_spec, P(), P(), P("dp", None, "mp"), P(), P("dp", "mp"),
            P(), P(), P(), P(), P("expert", None, ("dp", "mp")), P("expert", ("dp", "mp")),
            P("expert", ("dp", "mp"), None), P("expert", ("dp", "mp")),
        ),
        out_specs=(
            token_spec, token_spec, P(), P(), P("dp", None, "mp"), P(), P("dp", "mp"),
            P(), P(), P(), P(), P("expert", None, ("dp", "mp")), P("expert", ("dp", "mp")),
            P("expert", ("dp", "mp"), None), P("expert", ("dp", "mp")),
        ),
        check_vma=False,
    )
```

profile of v0, /device:TPU:0, one launch (start us, length us, event | category | flops | bytes accessed | tf_op | source)
XLA Modules:
  0.0 388.0 jit_solution(5206591975251365082)
XLA Ops:
  2.6 5.1 %collective-permute-start.1 = (bf16[48,1536]{1,0:T(8,128)(2,1)S(1)}, bf16[48,1536]{1,0:T(8,128)(2,1)S(1)}, u32[]{:S(2)}, u32[]{:S(2)}) collective-permute-start(bf16[48,1536]{1,0:T(8,128)(2,1)S(1)} %fusion.103), channel_id=1, source_target_pairs={{0,6},{2,0},{4,2},{6,4},{1,7},{3,1},{5,3},{7,5},{8,14},{10,8},{12,... | collective-permute-start | bytes 442376 | tf_op jit(solution)/shard_map/ppermute | solution.py:51
  12.0 8.2 %collective-permute-done.2 = bf16[48,1536]{1,0:T(8,128)(2,1)S(1)} collective-permute-done((bf16[48,1536]{1,0:T(8,128)(2,1)S(1)}, bf16[48,1536]{1,0:T(8,128)(2,1)S(1)}, u32[]{:S(2)}, u32[]{:S(2)}) %collective-permute-start.2) | collective-permute-done | bytes 147488 | tf_op jit(solution)/shard_map/ppermute | solution.py:51
  24.8 12.2 %collective-permute-done.4 = bf16[4,48,1536]{2,1,0:T(8,128)(2,1)S(1)} collective-permute-done((bf16[4,48,1536]{2,1,0:T(8,128)(2,1)S(1)}, bf16[4,48,1536]{2,1,0:T(8,128)(2,1)S(1)}, u32[]{:S(2)}, u32[]{:S(2)}) %collective-permute-start.4) | collective-permute-done | bytes 589856 | tf_op jit(solution)/shard_map/ppermute | solution.py:38
  37.1 12.1 %collective-permute-done.5 = bf16[4,48,1536]{2,1,0:T(8,128)(2,1)S(1)} collective-permute-done((bf16[4,48,1536]{2,1,0:T(8,128)(2,1)S(1)}, bf16[4,48,1536]{2,1,0:T(8,128)(2,1)S(1)}, u32[]{:S(2)}, u32[]{:S(2)}) %collective-permute-start.5) | collective-permute-done | bytes 589856 | tf_op jit(solution)/shard_map/ppermute | solution.py:38
  57.3 3.5 fusion.127
  69.4 3.7 all-to-all-start
  77.9 11.9 %all-to-all-done = bf16[4,104,1536]{2,1,0:T(8,128)(2,1)S(1)} async-done(((bf16[4,104,1536]{2,1,0:T(8,128)(2,1)}), bf16[4,104,1536]{2,1,0:T(8,128)(2,1)S(1)}, u32[]{:S(2)}, u32[]{:S(2)}) %all-to-all-start) | async-done | bytes 1277984 | tf_op jit(solution)/shard_map/all_to_all | solution.py:164
  106.8 3.9 %collective-permute-done.9 = bf16[768,384]{1,0:T(8,128)(2,1)S(1)} collective-permute-done((bf16[768,384]{1,0:T(8,128)(2,1)}, bf16[768,384]{1,0:T(8,128)(2,1)S(1)}, u32[]{:S(2)}, u32[]{:S(2)}) %collective-permute-start.9) | collective-permute-done | bytes 589856 | tf_op jit(solution)/shard_map/ppermute | solution.py:51
  113.9 32.8 %collective-permute-done.11 = bf16[384,768]{1,0:T(8,128)(2,1)S(1)} collective-permute-done((bf16[384,768]{1,0:T(8,128)(2,1)}, bf16[384,768]{1,0:T(8,128)(2,1)S(1)}, u32[]{:S(2)}, u32[]{:S(2)}) %collective-permute-start.11) | collective-permute-done | bytes 589856 | tf_op jit(solution)/shard_map/ppermute | solution.py:51
  148.7 3.6 convert_reduce_fusion.6
  157.3 18.4 %collective-permute-done.17 = bf16[384,768]{1,0:T(8,128)(2,1)} collective-permute-done((bf16[384,768]{1,0:T(8,128)(2,1)}, bf16[384,768]{1,0:T(8,128)(2,1)}, u32[]{:S(2)}, u32[]{:S(2)}) %collective-permute-start.17) | collective-permute-done | bytes 589856 | tf_op jit(solution)/shard_map/ppermute | solution.py:51
  182.8 17.0 %collective-permute-done.14 = bf16[384,768]{1,0:T(8,128)(2,1)} collective-permute-done((bf16[384,768]{1,0:T(8,128)(2,1)}, bf16[384,768]{1,0:T(8,128)(2,1)}, u32[]{:S(2)}, u32[]{:S(2)}) %collective-permute-start.14) | collective-permute-done | bytes 589856 | tf_op jit(solution)/shard_map/ppermute | solution.py:51
  212.0 5.9 %collective-permute-start.38 = (f32[1,480]{1,0:T(1,128)}, f32[1,480]{1,0:T(1,128)S(1)}, u32[]{:S(2)}, u32[]{:S(2)}) collective-permute-start(f32[1,480]{1,0:T(1,128)} %pad_maximum_fusion.8), channel_id=1, source_target_pairs={{0,2},{2,4},{4,6},{6,0},{1,3},{3,5},{5,7},{7,1},{8,10},{10,12},{12... | collective-permute-start | bytes 5768 | tf_op jit(solution)/shard_map/ppermute | solution.py:51
  232.1 3.7 all-to-all-start.1
  242.6 19.9 %collective-permute-done.40 = f32[1,480]{1,0:T(1,128)S(1)} collective-permute-done((f32[1,480]{1,0:T(1,128)S(1)}, f32[1,480]{1,0:T(1,128)S(1)}, u32[]{:S(2)}, u32[]{:S(2)}) %collective-permute-start.40) | collective-permute-done | bytes 1952 | tf_op jit(solution)/shard_map/ppermute | solution.py:51
  262.5 13.4 %collective-permute-start.43 = (bf16[384,768]{1,0:T(8,128)(2,1)}, bf16[384,768]{1,0:T(8,128)(2,1)}, u32[]{:S(2)}, u32[]{:S(2)}) collective-permute-start(bf16[384,768]{1,0:T(8,128)(2,1)} %convolution_convert_fusion.2), channel_id=1, source_target_pairs={{0,6},{2,0},{4,2},{6,4},{1,7},{3,1},{5,3},{7,5},{8,14},{10,8},{12,... | collective-permute-start | bytes 1769480 | tf_op jit(solution)/shard_map/ppermute | solution.py:51
  277.1 21.7 %collective-permute-start.42 = (bf16[384,768]{1,0:T(8,128)(2,1)}, bf16[384,768]{1,0:T(8,128)(2,1)}, u32[]{:S(2)}, u32[]{:S(2)}) collective-permute-start(bf16[384,768]{1,0:T(8,128)(2,1)} %convolution_convert_fusion.3), channel_id=1, source_target_pairs={{0,4},{2,6},{4,0},{6,2},{1,5},{3,7},{5,1},{7,3},{8,12},{10,14},{12... | collective-permute-start | bytes 1769480 | tf_op jit(solution)/shard_map/ppermute | solution.py:51
  298.8 3.5 fusion.15
  329.2 6.3 %collective-permute-done.42 = bf16[384,768]{1,0:T(8,128)(2,1)} collective-permute-done((bf16[384,768]{1,0:T(8,128)(2,1)}, bf16[384,768]{1,0:T(8,128)(2,1)}, u32[]{:S(2)}, u32[]{:S(2)}) %collective-permute-start.42) | collective-permute-done | bytes 589856 | tf_op jit(solution)/shard_map/ppermute | solution.py:51
  335.6 3.3 fusion.18
  338.9 14.5 %collective-permute-done.22 = f32[11,768]{1,0:T(8,128)S(1)} collective-permute-done((f32[11,768]{1,0:T(8,128)S(1)}, f32[11,768]{1,0:T(8,128)S(1)}, u32[]{:S(2)}, u32[]{:S(2)}) %collective-permute-start.22) | collective-permute-done | bytes 33824 | tf_op jit(solution)/shard_map/ppermute | solution.py:45
  357.6 4.1 %collective-permute-done.24 = f32[11,768]{1,0:T(8,128)S(1)} collective-permute-done((f32[11,768]{1,0:T(8,128)S(1)}, f32[11,768]{1,0:T(8,128)S(1)}, u32[]{:S(2)}, u32[]{:S(2)}) %collective-permute-start.24) | collective-permute-done | bytes 33824 | tf_op jit(solution)/shard_map/ppermute | solution.py:45
  370.7 4.2 %collective-permute-done.30 = bf16[48,1536]{1,0:T(8,128)(2,1)S(1)} collective-permute-done((bf16[48,1536]{1,0:T(8,128)(2,1)S(1)}, bf16[48,1536]{1,0:T(8,128)(2,1)S(1)}, u32[]{:S(2)}, u32[]{:S(2)}) %collective-permute-start.30) | collective-permute-done | bytes 147488 | tf_op jit(solution)/shard_map/ppermute | solution.py:51
  380.5 5.4 %collective-permute-done.33 = bf16[48,1536]{1,0:T(8,128)(2,1)S(1)} collective-permute-done((bf16[48,1536]{1,0:T(8,128)(2,1)S(1)}, bf16[48,1536]{1,0:T(8,128)(2,1)S(1)}, u32[]{:S(2)}, u32[]{:S(2)}) %collective-permute-start.33) | collective-permute-done | bytes 147488 | tf_op jit(solution)/shard_map/ppermute | solution.py:38
  (359 shorter events, 147.5 us)
Async XLA Ops:
  22.3 27.0 %collective-permute-start.5 = (bf16[4,48,1536]{2,1,0:T(8,128)(2,1)S(1)}, bf16[4,48,1536]{2,1,0:T(8,128)(2,1)S(1)}, u32[]{:S(2)}, u32[]{:S(2)}) collective-permute-start(bf16[4,48,1536]{2,1,0:T(8,128)(2,1)S(1)} %get-tuple-element.65), channel_id=1, source_target_pairs={{0,16},{8,24},{16,0},{24,8},{1,17},{9,25},{17,1},{25,9},{2,18},{10... | collective-permute-start | bytes 1769480 | tf_op jit(solution)/shard_map/ppermute | solution.py:38
  23.8 25.5 %collective-permute-start.6 = (bf16[4,48,1536]{2,1,0:T(8,128)(2,1)S(1)}, bf16[4,48,1536]{2,1,0:T(8,128)(2,1)S(1)}, u32[]{:S(2)}, u32[]{:S(2)}) collective-permute-start(bf16[4,48,1536]{2,1,0:T(8,128)(2,1)S(1)} %get-tuple-element.65), channel_id=1, source_target_pairs={{0,24},{8,16},{16,8},{24,0},{1,25},{9,17},{17,9},{25,1},{2,26},{10... | collective-permute-start | bytes 1769480 | tf_op jit(solution)/shard_map/ppermute | solution.py:38
  69.4 20.3 %all-to-all-start = ((bf16[4,104,1536]{2,1,0:T(8,128)(2,1)}), bf16[4,104,1536]{2,1,0:T(8,128)(2,1)S(1)}, u32[]{:S(2)}, u32[]{:S(2)}) async-start(bf16[4,104,1536]{2,1,0:T(8,128)(2,1)} %bitcast.25), calls=%async_computation | async-start | bytes 2555904 | tf_op jit(solution)/shard_map/all_to_all | solution.py:164
  73.6 18.7 %collective-permute-start.16 = (bf16[1,480]{1,0:T(2,128)(2,1)S(1)}, bf16[1,480]{1,0:T(2,128)(2,1)}, u32[]{:S(2)}, u32[]{:S(2)}) collective-permute-start(bf16[1,480]{1,0:T(2,128)(2,1)S(1)} %constant_dynamic-update-slice_fusion.1), channel_id=1, source_target_pairs={{0,2},{2,4},{4,6},{6,0},{1,3},{3,5},{5,7},{7,1},{8,10},{10,12},{12... | collective-permute-start | bytes 2888 | tf_op jit(solution)/shard_map/ppermute | solution.py:51
  94.7 60.5 %collective-permute-start.15 = (bf16[768,384]{1,0:T(8,128)(2,1)}, bf16[768,384]{1,0:T(8,128)(2,1)}, u32[]{:S(2)}, u32[]{:S(2)}) collective-permute-start(bf16[768,384]{1,0:T(8,128)(2,1)} %bitcast.261), channel_id=1, source_target_pairs={{0,2},{2,4},{4,6},{6,0},{1,3},{3,5},{5,7},{7,1},{8,10},{10,12},{12... | collective-permute-start | bytes 1769480 | tf_op jit(solution)/shard_map/ppermute | solution.py:51
  96.3 84.4 %collective-permute-start.12 = (bf16[768,384]{1,0:T(8,128)(2,1)}, bf16[768,384]{1,0:T(8,128)(2,1)}, u32[]{:S(2)}, u32[]{:S(2)}) collective-permute-start(bf16[768,384]{1,0:T(8,128)(2,1)} %bitcast.262), channel_id=1, source_target_pairs={{0,4},{2,6},{4,0},{6,2},{1,5},{3,7},{5,1},{7,3},{8,12},{10,14},{12... | collective-permute-start | bytes 1769480 | tf_op jit(solution)/shard_map/ppermute | solution.py:51
  99.0 47.7 %collective-permute-start.11 = (bf16[384,768]{1,0:T(8,128)(2,1)}, bf16[384,768]{1,0:T(8,128)(2,1)S(1)}, u32[]{:S(2)}, u32[]{:S(2)}) collective-permute-start(bf16[384,768]{1,0:T(8,128)(2,1)} %bitcast.7), channel_id=1, source_target_pairs={{0,6},{2,0},{4,2},{6,4},{1,7},{3,1},{5,3},{7,5},{8,14},{10,8},{12,... | collective-permute-start | bytes 1769480 | tf_op jit(solution)/shard_map/ppermute | solution.py:51
  102.2 97.6 %collective-permute-start.14 = (bf16[384,768]{1,0:T(8,128)(2,1)}, bf16[384,768]{1,0:T(8,128)(2,1)}, u32[]{:S(2)}, u32[]{:S(2)}) collective-permute-start(bf16[384,768]{1,0:T(8,128)(2,1)} %bitcast.7), channel_id=1, source_target_pairs={{0,4},{2,6},{4,0},{6,2},{1,5},{3,7},{5,1},{7,3},{8,12},{10,14},{12... | collective-permute-start | bytes 1769480 | tf_op jit(solution)/shard_map/ppermute | solution.py:51
  110.7 65.1 %collective-permute-start.17 = (bf16[384,768]{1,0:T(8,128)(2,1)}, bf16[384,768]{1,0:T(8,128)(2,1)}, u32[]{:S(2)}, u32[]{:S(2)}) collective-permute-start(bf16[384,768]{1,0:T(8,128)(2,1)} %bitcast.7), channel_id=1, source_target_pairs={{0,2},{2,4},{4,6},{6,0},{1,3},{3,5},{5,7},{7,1},{8,10},{10,12},{12... | collective-permute-start | bytes 1769480 | tf_op jit(solution)/shard_map/ppermute | solution.py:51
  210.8 19.3 %collective-permute-start.18 = (bf16[416,1536]{1,0:T(8,128)(2,1)S(1)}, bf16[416,1536]{1,0:T(8,128)(2,1)S(1)}, u32[]{:S(2)}, u32[]{:S(2)}) collective-permute-start(bf16[416,1536]{1,0:T(8,128)(2,1)S(1)} %fusion.5), channel_id=1, source_target_pairs={{0,1},{1,0},{2,3},{3,2},{4,5},{5,4},{6,7},{7,6},{8,9},{9,8},{10,11... | collective-permute-start | bytes 3833864 | tf_op jit(solution)/shard_map/ppermute | solution.py:30
  212.0 23.9 %collective-permute-start.38 = (f32[1,480]{1,0:T(1,128)}, f32[1,480]{1,0:T(1,128)S(1)}, u32[]{:S(2)}, u32[]{:S(2)}) collective-permute-start(f32[1,480]{1,0:T(1,128)} %pad_maximum_fusion.8), channel_id=1, source_target_pairs={{0,2},{2,4},{4,6},{6,0},{1,3},{3,5},{5,7},{7,1},{8,10},{10,12},{12... | collective-permute-start | bytes 5768 | tf_op jit(solution)/shard_map/ppermute | solution.py:51
  218.5 23.4 %collective-permute-start.39 = (f32[1,480]{1,0:T(1,128)}, f32[1,480]{1,0:T(1,128)S(1)}, u32[]{:S(2)}, u32[]{:S(2)}) collective-permute-start(f32[1,480]{1,0:T(1,128)} %pad_maximum_fusion.9), channel_id=1, source_target_pairs={{0,4},{2,6},{4,0},{6,2},{1,5},{3,7},{5,1},{7,3},{8,12},{10,14},{12... | collective-permute-start | bytes 5768 | tf_op jit(solution)/shard_map/ppermute | solution.py:51
  220.2 56.9 %collective-permute-start.37 = (bf16[768,384]{1,0:T(8,128)(2,1)}, bf16[768,384]{1,0:T(8,128)(2,1)}, u32[]{:S(2)}, u32[]{:S(2)}) collective-permute-start(bf16[768,384]{1,0:T(8,128)(2,1)} %convolution_convert_fusion.5), channel_id=1, source_target_pairs={{0,6},{2,0},{4,2},{6,4},{1,7},{3,1},{5,3},{7,5},{8,14},{10,8},{12,... | collective-permute-start | bytes 1769480 | tf_op jit(solution)/shard_map/ppermute | solution.py:51
  224.9 73.9 %collective-permute-start.35 = (bf16[768,384]{1,0:T(8,128)(2,1)}, bf16[768,384]{1,0:T(8,128)(2,1)}, u32[]{:S(2)}, u32[]{:S(2)}) collective-permute-start(bf16[768,384]{1,0:T(8,128)(2,1)} %convolution_convert_fusion.7), channel_id=1, source_target_pairs={{0,2},{2,4},{4,6},{6,0},{1,3},{3,5},{5,7},{7,1},{8,10},{10,12},{12... | collective-permute-start | bytes 1769480 | tf_op jit(solution)/shard_map/ppermute | solution.py:51
  230.1 68.7 %collective-permute-start.36 = (bf16[768,384]{1,0:T(8,128)(2,1)}, bf16[768,384]{1,0:T(8,128)(2,1)}, u32[]{:S(2)}, u32[]{:S(2)}) collective-permute-start(bf16[768,384]{1,0:T(8,128)(2,1)} %convolution_convert_fusion.6), channel_id=1, source_target_pairs={{0,4},{2,6},{4,0},{6,2},{1,5},{3,7},{5,1},{7,3},{8,12},{10,14},{12... | collective-permute-start | bytes 1769480 | tf_op jit(solution)/shard_map/ppermute | solution.py:51
  232.1 70.3 %all-to-all-start.1 = ((bf16[4,104,1536]{2,1,0:T(8,128)(2,1)}), bf16[4,104,1536]{2,1,0:T(8,128)(2,1)S(1)}, u32[]{:S(2)}, u32[]{:S(2)}) async-start(bf16[4,104,1536]{2,1,0:T(8,128)(2,1)} %bitcast.31), calls=%async_computation.1 | async-start | bytes 2555904 | tf_op jit(solution)/shard_map/all_to_all | solution.py:207
  235.8 26.7 %collective-permute-start.40 = (f32[1,480]{1,0:T(1,128)S(1)}, f32[1,480]{1,0:T(1,128)S(1)}, u32[]{:S(2)}, u32[]{:S(2)}) collective-permute-start(f32[1,480]{1,0:T(1,128)S(1)} %pad_maximum_fusion.10), channel_id=1, source_target_pairs={{0,6},{2,0},{4,2},{6,4},{1,7},{3,1},{5,3},{7,5},{8,14},{10,8},{12,... | collective-permute-start | bytes 5768 | tf_op jit(solution)/shard_map/ppermute | solution.py:51
  241.9 84.4 %collective-permute-start.41 = (bf16[384,768]{1,0:T(8,128)(2,1)}, bf16[384,768]{1,0:T(8,128)(2,1)}, u32[]{:S(2)}, u32[]{:S(2)}) collective-permute-start(bf16[384,768]{1,0:T(8,128)(2,1)} %convolution_convert_fusion.4), channel_id=1, source_target_pairs={{0,2},{2,4},{4,6},{6,0},{1,3},{3,5},{5,7},{7,1},{8,10},{10,12},{12... | collective-permute-start | bytes 1769480 | tf_op jit(solution)/shard_map/ppermute | solution.py:51
  262.5 65.3 %collective-permute-start.43 = (bf16[384,768]{1,0:T(8,128)(2,1)}, bf16[384,768]{1,0:T(8,128)(2,1)}, u32[]{:S(2)}, u32[]{:S(2)}) collective-permute-start(bf16[384,768]{1,0:T(8,128)(2,1)} %convolution_convert_fusion.2), channel_id=1, source_target_pairs={{0,6},{2,0},{4,2},{6,4},{1,7},{3,1},{5,3},{7,5},{8,14},{10,8},{12,... | collective-permute-start | bytes 1769480 | tf_op jit(solution)/shard_map/ppermute | solution.py:51
  277.1 58.5 %collective-permute-start.42 = (bf16[384,768]{1,0:T(8,128)(2,1)}, bf16[384,768]{1,0:T(8,128)(2,1)}, u32[]{:S(2)}, u32[]{:S(2)}) collective-permute-start(bf16[384,768]{1,0:T(8,128)(2,1)} %convolution_convert_fusion.3), channel_id=1, source_target_pairs={{0,4},{2,6},{4,0},{6,2},{1,5},{3,7},{5,1},{7,3},{8,12},{10,14},{12... | collective-permute-start | bytes 1769480 | tf_op jit(solution)/shard_map/ppermute | solution.py:51
  324.2 37.7 %collective-permute-start.26 = (bf16[4,48,1536]{2,1,0:T(8,128)(2,1)S(1)}, bf16[4,48,1536]{2,1,0:T(8,128)(2,1)S(1)}, u32[]{:S(2)}, u32[]{:S(2)}) collective-permute-start(bf16[4,48,1536]{2,1,0:T(8,128)(2,1)S(1)} %get-tuple-element.66), channel_id=1, source_target_pairs={{0,8},{8,0},{16,24},{24,16},{1,9},{9,1},{17,25},{25,17},{2,10},{10... | collective-permute-start | bytes 1769480 | tf_op jit(solution)/shard_map/ppermute | solution.py:38
  325.6 36.2 %collective-permute-start.27 = (bf16[4,48,1536]{2,1,0:T(8,128)(2,1)S(1)}, bf16[4,48,1536]{2,1,0:T(8,128)(2,1)S(1)}, u32[]{:S(2)}, u32[]{:S(2)}) collective-permute-start(bf16[4,48,1536]{2,1,0:T(8,128)(2,1)S(1)} %get-tuple-element.67), channel_id=1, source_target_pairs={{0,16},{8,24},{16,0},{24,8},{1,17},{9,25},{17,1},{25,9},{2,18},{10... | collective-permute-start | bytes 1769480 | tf_op jit(solution)/shard_map/ppermute | solution.py:38
  326.3 35.5 %collective-permute-start.28 = (bf16[4,48,1536]{2,1,0:T(8,128)(2,1)S(1)}, bf16[4,48,1536]{2,1,0:T(8,128)(2,1)S(1)}, u32[]{:S(2)}, u32[]{:S(2)}) collective-permute-start(bf16[4,48,1536]{2,1,0:T(8,128)(2,1)S(1)} %get-tuple-element.68), channel_id=1, source_target_pairs={{0,24},{8,16},{16,8},{24,0},{1,25},{9,17},{17,9},{25,1},{2,26},{10... | collective-permute-start | bytes 1769480 | tf_op jit(solution)/shard_map/ppermute | solution.py:38
  327.8 25.6 %collective-permute-start.22 = (f32[11,768]{1,0:T(8,128)S(1)}, f32[11,768]{1,0:T(8,128)S(1)}, u32[]{:S(2)}, u32[]{:S(2)}) collective-permute-start(f32[11,768]{1,0:T(8,128)S(1)} %add.420), channel_id=1, source_target_pairs={{0,8},{8,0},{16,24},{24,16},{1,9},{9,1},{17,25},{25,17},{2,10},{10... | collective-permute-start | bytes 101384 | tf_op jit(solution)/shard_map/ppermute | solution.py:45
  (86 other events, 1109.8 us)
where the time goes:
time: 393 us; the launch traced here: 388 us
  waiting for transfers between devices  179 us (46%)
  starting transfers between devices  96.8 us (25%)
  matrix products  71.9 us (18%)
  local copies, waits for them, and re-layouts  22.8 us (6%)
  other arithmetic  15.2 us (4%)
    ppermute x24, waiting for transfers between devices, to_owner(): lax.ppermute(chunk, 'dp', [(z, (z + k) % count) for z in range(count)])  115 us
    ppermute x24, starting transfers between devices, to_owner(): lax.ppermute(chunk, 'dp', [(z, (z + k) % count) for z in range(count)])  74.8 us
    dot_general x44, matrix products, mm(): return jnp.einsum(spec, a, b, preferred_element_type=F32)  67.6 us
    ppermute x9, waiting for transfers between devices, across(): return lax.ppermute(value, 'expert', [(e, e ^ j) for e in range(count)])  29.8 us
    ppermute x5, waiting for transfers between devices, sum_all(): lax.ppermute(value, axis, [(i, i ^ step) for i in range(count)])  21.4 us
    all_to_all x1, waiting for transfers between devices, on_device(): lax.all_to_all(send, 'expert', split_axis=0, concat_axis=0, tiled=True)  11.9 us
    ppermute x9, starting transfers between devices, across(): return lax.ppermute(value, 'expert', [(e, e ^ j) for e in range(count)])  10.7 us
  transfers between devices with their start and end apart: 46, of which 20 were waited for; matrix products, arithmetic and copies ran while one was open for 19% of the time, Pallas kernels for 0%

commit v1 on v0

--- a/solution.py
+++ b/solution.py
@@ -102,11 +102,19 @@
     )
     part = shard.shape[0] // expert_axis
     mine = lax.dynamic_slice_in_dim(shard, expert_index * part, part, 0)
-    column = jnp.stack(from_axis(mine, dp_count))
-    column, up_own, down_own = lax.optimization_barrier((column, up_weight[0], down_weight[0]))
+    ff_part = up_weight.shape[2]
+    bias_part = down_bias.shape[1]
+    bias_own = jnp.concatenate([up_bias, down_bias], axis=1)
+    bias_own = jnp.pad(bias_own, ((0, 7), (0, 4 * local - ff_part - bias_part)))
+    column = jnp.stack(from_axis(jnp.concatenate([mine, bias_own]), dp_count))
     column = lax.dynamic_slice_in_dim(
         jnp.concatenate([column, column]), lax.rem(dp_count - dp_index, dp_count), dp_count, 0
     )
+    up_bias_row = column[:, part, :ff_part].astype(F32).reshape(1, -1)
+    down_bias_row = column[:, part, ff_part : ff_part + bias_part].astype(F32)
+    column = column[:, :part]
+    up_full = lax.all_gather(up_weight[0], "dp", axis=1, tiled=True)
+    down_full = lax.all_gather(down_weight[0], "dp", axis=0, tiled=True)
     attn_full = jnp.zeros((dp_count, expert_axis) + mine.shape, BF)
     for j in range(expert_axis):
         piece = across(column, j, expert_axis) if j else column
@@ -117,13 +125,6 @@
     input_full, output_full = attn_full[:, : 3 * local], attn_full[:, 3 * local :]
 
     other_tokens = swap(tokens)
-    ff_part = up_weight.shape[2]
-    bias_part = down_bias.shape[1]
-    ups = from_axis(up_own, dp_count)
-    downs = from_axis(down_own, dp_count)
-    bias_own = jnp.concatenate([up_bias, down_bias], axis=1)
-    biases = from_axis(bias_own, dp_count)
-
     flat_routes = jnp.concatenate([routes[:, 0], routes[:, 1]])
     expert_ids = jnp.arange(experts, dtype=jnp.int32)
     one_hot = flat_routes[:, None] == expert_ids[None, :]
@@ -167,41 +168,33 @@
     both = jnp.concatenate([received, swap(received)], axis=0)
     slab, slab_grad = both[:, :width], both[:, width:]
 
-    produced = grad_slab = 0.0
-    up_sums, down_sums, bias_sums = [], [], []
+    pre = mm("td,df->tf", slab, up_full) + up_bias_row
+    cdf = 0.5 * (1.0 + lax.erf(pre * (0.5**0.5)))
+    slope = cdf + pre * (jnp.exp(-0.5 * pre * pre) * 0.3989422804014327)
+    hidden = (pre * cdf).astype(BF)
+    bias_row = lax.dynamic_update_slice_in_dim(
+        jnp.zeros((dp_count, mp_count, bias_part), F32), down_bias_row[:, None], mp_index, 1
+    )
+    produced = mm("tf,fd->td", hidden, down_full) + bias_row.reshape(1, -1)
+    grad_pre = (mm("td,fd->tf", slab_grad, down_full) * slope).astype(BF)
+    grad_slab = mm("tf,df->td", grad_pre, up_full)
+    down_grad = mm("tf,td->fd", hidden, slab_grad).reshape(dp_count, ff_part, width)
+    up_grad = mm("tf,td->fd", grad_pre, slab).reshape(dp_count, ff_part, width)
     column_sum = jnp.sum(slab_grad, axis=0, dtype=F32).reshape(dp_count, mp_count, bias_part)
-    column_sum = lax.dynamic_index_in_dim(column_sum, mp_index, 1, keepdims=False)
-    bias_row = jnp.zeros((dp_count, mp_count, bias_part), F32)
-    for k in range(dp_count):
-        owner = lax.rem(dp_index + k, dp_count)
-        bias_k = biases[k].astype(F32)
-        bias_row = lax.dynamic_update_slice(
-            bias_row, bias_k[:, None, ff_part:], (owner, mp_index, jnp.int32(0))
-        )
-        pre = mm("td,df->tf", slab, ups[k]) + bias_k[:, :ff_part]
-        cdf = 0.5 * (1.0 + lax.erf(pre * (0.5**0.5)))
-        slope = cdf + pre * (jnp.exp(-0.5 * pre * pre) * 0.3989422804014327)
-        hidden = (pre * cdf).astype(BF)
-        produced = produced + mm("tf,fd->td", hidden, downs[k])
-        grad_pre = (mm("td,fd->tf", slab_grad, downs[k]) * slope).astype(BF)
-        grad_slab = grad_slab + mm("tf,df->td", grad_pre, ups[k])
-        down_part = mm("tf,td->fd", hidden, slab_grad)
-        up_part = mm("td,tf->df", slab, grad_pre)
-        bias_grad = jnp.concatenate(
-            [
-                jnp.sum(grad_pre, axis=0, dtype=F32)[None, :],
-                lax.dynamic_index_in_dim(column_sum, owner, 0),
-            ],
-            axis=1,
-        )
-        if k:
-            down_part = to_owner(down_part.astype(BF), k, dp_count).astype(F32)
-            up_part = to_owner(up_part.astype(BF), k, dp_count).astype(F32)
-            bias_grad = to_owner(bias_grad, k, dp_count)
-        down_sums.append(down_part)
-        up_sums.append(up_part)
-        bias_sums.append(bias_grad)
-    produced = produced + bias_row.reshape(1, -1)
+    bias_grad = jnp.concatenate(
+        [
+            jnp.sum(grad_pre, axis=0, dtype=F32).reshape(dp_count, ff_part),
+            lax.dynamic_index_in_dim(column_sum, mp_index, 1, keepdims=False),
+        ],
+        axis=1,
+    )
+    bias_grad = jnp.pad(
+        bias_grad[:, None], ((0, 0), (0, 7), (0, width - ff_part - bias_part))
+    )
+    payload = jnp.concatenate([g.astype(BF) for g in (down_grad, up_grad, bias_grad)], axis=1)
+    expert_grad = lax.psum_scatter(
+        payload.reshape(-1, width), "dp", scatter_dimension=0, tiled=True
+    ).astype(F32)
     partial = jnp.concatenate([produced, grad_slab], axis=1)
     back = (partial[:count] + swap(partial[count:].astype(BF)).astype(F32)).astype(BF)
     returned = lax.all_to_all(
@@ -269,7 +262,7 @@
         ]
     )
     small = sum_all(small)
-    bias_total = sum(bias_sums)
+    bias_total = expert_grad[2 * ff_part :][:1]
     return (
         result,
         tokens_grad,
@@ -282,10 +275,10 @@
         small[5],
         small[6],
         small[7:].T,
-        sum(up_sums)[None],
+        expert_grad[ff_part : 2 * ff_part].T[None],
         bias_total[:, :ff_part],
-        sum(down_sums)[None],
-        bias_total[:, ff_part:],
+        expert_grad[None, :ff_part],
+        bias_total[:, ff_part : ff_part + bias_part],
     )
 
 

time: 393 us -> 291 us (0.74); the launches traced: 388 us -> 290 us
  waiting for transfers between devices: 179 us -> 116 us
  starting transfers between devices: 96.8 us -> 34.7 us
  blocking collectives: 0 us -> 20.3 us
  matrix products: 71.9 us -> 56.1 us
  between operations: 2.09 us -> 14.8 us
  other arithmetic: 15.2 us -> 22.3 us
    ppermute x24 -> x6, waiting for transfers between devices: 115 us -> 27 us  [to_owner(): lax.ppermute(chunk, 'dp', [(z, (z + k) % count) for z in range(count)])]
    ppermute x24 -> x6, starting transfers between devices: 74.8 us -> 10 us  [to_owner(): lax.ppermute(chunk, 'dp', [(z, (z + k) % count) for z in range(count)])]
    all_to_all x0 -> x1, blocking collectives: none -> 20.3 us  [on_device(): lax.all_to_all(send, 'expert', split_axis=0, concat_axis=0, tiled=True)]
    all_gather x0 -> x2, waiting for transfers between devices: none -> 16.7 us  [the longest x1 16.7 us: on_device(): down_full = lax.all_gather(down_weight[0], 'dp', axis=0, tiled=True)]
    dot_general x44 -> x26, matrix products: 67.6 us -> 52.8 us  [mm(): return jnp.einsum(spec, a, b, preferred_element_type=F32)]
    all_to_all x1 -> x0, waiting for transfers between devices: 11.9 us -> none  [on_device(): lax.all_to_all(send, 'expert', split_axis=0, concat_axis=0, tiled=True)]
    ppermute x5, waiting for transfers between devices: 21.4 us -> 32.2 us  [sum_all(): lax.ppermute(value, axis, [(i, i ^ step) for i in range(count)])]
    all_to_all x1, waiting for transfers between devices: 0.01 us -> 9.33 us  [on_device(): lax.all_to_all(back.reshape(expert_axis, -1, 2 * width), 'expert', split_...]
  transfers between devices with their start and end apart: 46 -> 30, of which waited for: 20 -> 19; matrix products, arithmetic and copies ran while one was open for 19% -> 27% of each run, Pallas kernels for 0% -> 0%
where the time goes in v1:
time: 291 us; the launch traced here: 290 us
  waiting for transfers between devices  116 us (40%)
  matrix products  56.1 us (19%)
  starting transfers between devices  34.7 us (12%)
  local copies, waits for them, and re-layouts  25.8 us (9%)
  other arithmetic  22.3 us (8%)
  blocking collectives  20.3 us (7%)
  between operations  14.8 us (5%)
    dot_general x26, matrix products, mm(): return jnp.einsum(spec, a, b, preferred_element_type=F32)  52.8 us
    ppermute x5, waiting for transfers between devices, sum_all(): lax.ppermute(value, axis, [(i, i ^ step) for i in range(count)])  32.2 us
    ppermute x9, waiting for transfers between devices, across(): return lax.ppermute(value, 'expert', [(e, e ^ j) for e in range(count)])  28 us
    ppermute x6, waiting for transfers between devices, to_owner(): lax.ppermute(chunk, 'dp', [(z, (z + k) % count) for z in range(count)])  27 us
    all_to_all x1, blocking collectives, on_device(): lax.all_to_all(send, 'expert', split_axis=0, concat_axis=0, tiled=True)  20.3 us
    all_gather x1, waiting for transfers between devices, on_device(): down_full = lax.all_gather(down_weight[0], 'dp', axis=0, tiled=True)  16.7 us
    ppermute x9, starting transfers between devices, across(): return lax.ppermute(value, 'expert', [(e, e ^ j) for e in range(count)])  10.7 us
    ppermute x6, starting transfers between devices, to_owner(): lax.ppermute(chunk, 'dp', [(z, (z + k) % count) for z in range(count)])  10 us
  transfers between devices with their start and end apart: 30, of which 19 were waited for; matrix products, arithmetic and copies ran while one was open for 27% of the time, Pallas kernels for 0%

profile of v1, /device:TPU:0, one launch (start us, length us, event | category | flops | bytes accessed | tf_op | source)
XLA Modules:
  0.0 290.0 jit_solution(16975007386578904184)
XLA Ops:
  10.6 4.1 %collective-permute-start.2 = (bf16[56,1536]{1,0:T(8,128)(2,1)S(1)}, bf16[56,1536]{1,0:T(8,128)(2,1)S(1)}, u32[]{:S(2)}, u32[]{:S(2)}) collective-permute-start(bf16[56,1536]{1,0:T(8,128)(2,1)S(1)} %pad_maximum_fusion.7), channel_id=1, source_target_pairs={{0,4},{2,6},{4,0},{6,2},{1,5},{3,7},{5,1},{7,3},{8,12},{10,14},{12... | collective-permute-start | bytes 516104 | tf_op jit(solution)/shard_map/ppermute | solution.py:51
  17.0 8.6 %collective-permute-done.1 = bf16[56,1536]{1,0:T(8,128)(2,1)S(1)} collective-permute-done((bf16[56,1536]{1,0:T(8,128)(2,1)S(1)}, bf16[56,1536]{1,0:T(8,128)(2,1)S(1)}, u32[]{:S(2)}, u32[]{:S(2)}) %collective-permute-start.1) | collective-permute-done | bytes 172064 | tf_op jit(solution)/shard_map/ppermute | solution.py:51
  25.7 6.2 %collective-permute-done.3 = bf16[56,1536]{1,0:T(8,128)(2,1)S(1)} collective-permute-done((bf16[56,1536]{1,0:T(8,128)(2,1)S(1)}, bf16[56,1536]{1,0:T(8,128)(2,1)S(1)}, u32[]{:S(2)}, u32[]{:S(2)}) %collective-permute-start.3) | collective-permute-done | bytes 172064 | tf_op jit(solution)/shard_map/ppermute | solution.py:51
  36.4 13.6 %collective-permute-done.4 = bf16[4,48,1536]{2,1,0:T(8,128)(2,1)S(1)} collective-permute-done((bf16[4,48,1536]{2,1,0:T(8,128)(2,1)S(1)}, bf16[4,48,1536]{2,1,0:T(8,128)(2,1)S(1)}, u32[]{:S(2)}, u32[]{:S(2)}) %collective-permute-start.4) | collective-permute-done | bytes 589856 | tf_op jit(solution)/shard_map/ppermute | solution.py:38
  50.1 8.0 %collective-permute-done.6 = bf16[4,48,1536]{2,1,0:T(8,128)(2,1)S(1)} collective-permute-done((bf16[4,48,1536]{2,1,0:T(8,128)(2,1)S(1)}, bf16[4,48,1536]{2,1,0:T(8,128)(2,1)S(1)}, u32[]{:S(2)}, u32[]{:S(2)}) %collective-permute-start.6) | collective-permute-done | bytes 589856 | tf_op jit(solution)/shard_map/ppermute | solution.py:38
  74.5 20.3 %all_to_all.10 = bf16[4,104,1536]{2,1,0:T(8,128)(2,1)S(1)} all-to-all(bf16[4,104,1536]{2,1,0:T(8,128)(2,1)S(1)} %bitcast.205), channel_id=1, replica_groups=mesh['expert'=4,'dp'=4,'mp'=2] {'expert'}, dimensions={0} | all-to-all | bytes 2555904 | tf_op jit(solution)/shard_map/all_to_all | solution.py:165
  97.8 7.3 %multiply_convert_fusion = (bf16[832,1536]{1,0:T(8,128)(2,1)}, f32[832,1536]{1,0:T(8,128)}) fusion(f32[1536]{0:T(1024)S(1)} %reshape.230, bf16[1,768,1536]{2,1,0:T(8,128)(2,1)} %all-gather.5.cloned.1.call-done, bf16[416,1536]{1,0:T(8,128)(2,1)S(1)} %bitcast.207, bf16[416,1536]{1,0:T(8,128)(2,1)S(1)} %collective-permute-done.8), kind=kOutput, calls=%fused_computation.12 | convolution fusion | flops 1973157888 | bytes 12589056 | tf_op jit(solution)/shard_map/td,df->tf/dot_general | solution.py:13
  105.2 16.7 %all-gather.7.cloned.1.call-done = bf16[1,1536,768]{2,1,0:T(8,128)(2,1)} async-done(((bf16[1,384,768]{2,1,0:T(8,128)(2,1)}), bf16[1,1536,768]{2,1,0:T(8,128)(2,1)}) %all-gather.7.cloned.1.call-update) | async-done | bytes 2359312 | tf_op jit(solution)/shard_map/all_gather | solution.py:117
  121.8 7.8 %fusion.123 = (bf16[1536]{0:T(1024)(128)(2,1)}, bf16[832,1536]{1,0:T(8,128)(2,1)S(1)}) fusion(f32[832,1536]{1,0:T(8,128)} %get-tuple-element.101, f32[1536]{0:T(1024)S(1)} %reshape.230, bf16[1,1536,768]{2,1,0:T(8,128)(2,1)} %all-gather.7.cloned.1.call-done, bf16[416,1536]{1,0:T(8,128)(2,1)S(1)} %collective-permute-done.8, bf16[416,1536]{1,0:T(8,128)(2,1)S(1)} %bitcast.208), kind=kOutput, calls=%fused_computation.241 | convolution fusion | flops 1980824064 | bytes 12592128 | tf_op jit(solution)/shard_map/td,fd->tf/dot_general | solution.py:13
  139.1 6.3 %convolution_convert_fusion.1 = bf16[1536,768]{1,0:T(8,128)(2,1)} fusion(bf16[832,1536]{1,0:T(8,128)(2,1)} %get-tuple-element.100, bf16[416,1536]{1,0:T(8,128)(2,1)} %copy-done.24, bf16[416,1536]{1,0:T(8,128)(2,1)} %bitcast.209), kind=kOutput, calls=%fused_computation.22 | convolution fusion | flops 1966669824 | bytes 7471104 | tf_op jit(solution)/shard_map/tf,td->fd/dot_general | solution.py:13
  145.4 2.7 fusion.12
  148.1 3.8 %all-to-all-start.1 = ((bf16[4,104,1536]{2,1,0:T(8,128)(2,1)}), bf16[4,104,1536]{2,1,0:T(8,128)(2,1)S(1)}, u32[]{:S(2)}, u32[]{:S(2)}) async-start(bf16[4,104,1536]{2,1,0:T(8,128)(2,1)} %bitcast.212), calls=%async_computation.1 | async-start | bytes 2555904 | tf_op jit(solution)/shard_map/all_to_all | solution.py:200
  151.9 4.7 %convolution_convert_fusion = bf16[1536,768]{1,0:T(8,128)(2,1)S(1)} fusion(bf16[832,1536]{1,0:T(8,128)(2,1)} %copy-done.50, bf16[416,1536]{1,0:T(8,128)(2,1)S(1)} %bitcast.211, bf16[416,1536]{1,0:T(8,128)(2,1)} %copy-done.24), kind=kOutput, calls=%fused_computation.21 | convolution fusion | flops 1966669824 | bytes 7471104 | tf_op jit(solution)/shard_map/tf,td->fd/dot_general | solution.py:13
  159.2 9.3 %all-to-all-done.1 = bf16[4,104,1536]{2,1,0:T(8,128)(2,1)S(1)} async-done(((bf16[4,104,1536]{2,1,0:T(8,128)(2,1)}), bf16[4,104,1536]{2,1,0:T(8,128)(2,1)S(1)}, u32[]{:S(2)}, u32[]{:S(2)}) %all-to-all-start.1) | async-done | bytes 1277984 | tf_op jit(solution)/shard_map/all_to_all | solution.py:200
  204.8 21.4 %collective-permute-done.13 = f32[11,768]{1,0:T(8,128)S(1)} collective-permute-done((f32[11,768]{1,0:T(8,128)S(1)}, f32[11,768]{1,0:T(8,128)S(1)}, u32[]{:S(2)}, u32[]{:S(2)}) %collective-permute-start.13) | collective-permute-done | bytes 33824 | tf_op jit(solution)/shard_map/ppermute | solution.py:45
  227.7 2.6 collective-permute-done.14
  230.4 3.8 %collective-permute-start.15 = (f32[11,768]{1,0:T(8,128)S(1)}, f32[11,768]{1,0:T(8,128)S(1)}, u32[]{:S(2)}, u32[]{:S(2)}) collective-permute-start(f32[11,768]{1,0:T(8,128)S(1)} %add.281), channel_id=1, source_target_pairs={{0,2},{2,0},{4,6},{6,4},{1,3},{3,1},{5,7},{7,5},{8,10},{10,8},{12,... | collective-permute-start | bytes 101384 | tf_op jit(solution)/shard_map/ppermute | solution.py:45
  234.2 4.3 %collective-permute-done.15 = f32[11,768]{1,0:T(8,128)S(1)} collective-permute-done((f32[11,768]{1,0:T(8,128)S(1)}, f32[11,768]{1,0:T(8,128)S(1)}, u32[]{:S(2)}, u32[]{:S(2)}) %collective-permute-start.15) | collective-permute-done | bytes 33824 | tf_op jit(solution)/shard_map/ppermute | solution.py:45
  238.6 2.9 %collective-permute-start.16 = (f32[11,768]{1,0:T(8,128)S(1)}, f32[11,768]{1,0:T(8,128)S(1)}, u32[]{:S(2)}, u32[]{:S(2)}) collective-permute-start(f32[11,768]{1,0:T(8,128)S(1)} %add.282), channel_id=1, source_target_pairs={{0,4},{2,6},{4,0},{6,2},{1,5},{3,7},{5,1},{7,3},{8,12},{10,14},{12... | collective-permute-start | bytes 101384 | tf_op jit(solution)/shard_map/ppermute | solution.py:45
  243.4 3.8 %collective-permute-start.22 = (bf16[48,1536]{1,0:T(8,128)(2,1)S(1)}, bf16[48,1536]{1,0:T(8,128)(2,1)S(1)}, u32[]{:S(2)}, u32[]{:S(2)}) collective-permute-start(bf16[48,1536]{1,0:T(8,128)(2,1)S(1)} %get-tuple-element.82), channel_id=1, source_target_pairs={{0,6},{2,0},{4,2},{6,4},{1,7},{3,1},{5,3},{7,5},{8,14},{10,8},{12,... | collective-permute-start | bytes 442376 | tf_op jit(solution)/shard_map/ppermute | solution.py:51
  248.3 2.7 collective-permute-done.16
  251.0 4.3 %collective-permute-done.20 = bf16[48,1536]{1,0:T(8,128)(2,1)S(1)} collective-permute-done((bf16[48,1536]{1,0:T(8,128)(2,1)S(1)}, bf16[48,1536]{1,0:T(8,128)(2,1)S(1)}, u32[]{:S(2)}, u32[]{:S(2)}) %collective-permute-start.20) | collective-permute-done | bytes 147488 | tf_op jit(solution)/shard_map/ppermute | solution.py:51
  256.0 7.2 %collective-permute-done.21 = bf16[48,1536]{1,0:T(8,128)(2,1)S(1)} collective-permute-done((bf16[48,1536]{1,0:T(8,128)(2,1)S(1)}, bf16[48,1536]{1,0:T(8,128)(2,1)S(1)}, u32[]{:S(2)}, u32[]{:S(2)}) %collective-permute-start.21) | collective-permute-done | bytes 147488 | tf_op jit(solution)/shard_map/ppermute | solution.py:51
  269.0 6.2 %collective-permute-done.24 = bf16[48,1536]{1,0:T(8,128)(2,1)S(1)} collective-permute-done((bf16[48,1536]{1,0:T(8,128)(2,1)S(1)}, bf16[48,1536]{1,0:T(8,128)(2,1)S(1)}, u32[]{:S(2)}, u32[]{:S(2)}) %collective-permute-start.24) | collective-permute-done | bytes 147488 | tf_op jit(solution)/shard_map/ppermute | solution.py:38
  (284 shorter events, 96.6 us)
Async XLA Ops:
  7.2 90.0 %all-gather.5.cloned.1.call-start = ((), (), s32[]{:S(2)}) async-start(), calls=%async_computation.4 | async-start | bytes 2949120 | tf_op jit(solution)/shard_map/all_gather | solution.py:116
  8.0 113.9 %all-gather.7.cloned.1.call-start = ((), (), s32[]{:S(2)}) async-start(), calls=%async_computation.5 | async-start | bytes 2949120 | tf_op jit(solution)/shard_map/all_gather | solution.py:117
  10.6 15.0 %collective-permute-start.2 = (bf16[56,1536]{1,0:T(8,128)(2,1)S(1)}, bf16[56,1536]{1,0:T(8,128)(2,1)S(1)}, u32[]{:S(2)}, u32[]{:S(2)}) collective-permute-start(bf16[56,1536]{1,0:T(8,128)(2,1)S(1)} %pad_maximum_fusion.7), channel_id=1, source_target_pairs={{0,4},{2,6},{4,0},{6,2},{1,5},{3,7},{5,1},{7,3},{8,12},{10,14},{12... | collective-permute-start | bytes 516104 | tf_op jit(solution)/shard_map/ppermute | solution.py:51
  14.7 10.9 %collective-permute-start.1 = (bf16[56,1536]{1,0:T(8,128)(2,1)S(1)}, bf16[56,1536]{1,0:T(8,128)(2,1)S(1)}, u32[]{:S(2)}, u32[]{:S(2)}) collective-permute-start(bf16[56,1536]{1,0:T(8,128)(2,1)S(1)} %pad_maximum_fusion.7), channel_id=1, source_target_pairs={{0,6},{2,0},{4,2},{6,4},{1,7},{3,1},{5,3},{7,5},{8,14},{10,8},{12,... | collective-permute-start | bytes 516104 | tf_op jit(solution)/shard_map/ppermute | solution.py:51
  16.1 15.8 %collective-permute-start.3 = (bf16[56,1536]{1,0:T(8,128)(2,1)S(1)}, bf16[56,1536]{1,0:T(8,128)(2,1)S(1)}, u32[]{:S(2)}, u32[]{:S(2)}) collective-permute-start(bf16[56,1536]{1,0:T(8,128)(2,1)S(1)} %pad_maximum_fusion.7), channel_id=1, source_target_pairs={{0,2},{2,4},{4,6},{6,0},{1,3},{3,5},{5,7},{7,1},{8,10},{10,12},{12... | collective-permute-start | bytes 516104 | tf_op jit(solution)/shard_map/ppermute | solution.py:51
  16.7 19.1 %collective-permute-start = (bf16[197,768]{1,0:T(8,128)(2,1)S(1)}, bf16[197,768]{1,0:T(8,128)(2,1)S(1)}, u32[]{:S(2)}, u32[]{:S(2)}) collective-permute-start(bf16[197,768]{1,0:T(8,128)(2,1)S(1)} %copy-done.9), channel_id=1, source_target_pairs={{0,1},{1,0},{2,3},{3,2},{4,5},{5,4},{6,7},{7,6},{8,9},{9,8},{10,11... | collective-permute-start | bytes 907784 | tf_op jit(solution)/shard_map/ppermute | solution.py:30
  32.3 17.7 %collective-permute-start.5 = (bf16[4,48,1536]{2,1,0:T(8,128)(2,1)S(1)}, bf16[4,48,1536]{2,1,0:T(8,128)(2,1)S(1)}, u32[]{:S(2)}, u32[]{:S(2)}) collective-permute-start(bf16[4,48,1536]{2,1,0:T(8,128)(2,1)S(1)} %get-tuple-element.72), channel_id=1, source_target_pairs={{0,16},{8,24},{16,0},{24,8},{1,17},{9,25},{17,1},{25,9},{2,18},{10... | collective-permute-start | bytes 1769480 | tf_op jit(solution)/shard_map/ppermute | solution.py:38
  33.7 16.3 %collective-permute-start.4 = (bf16[4,48,1536]{2,1,0:T(8,128)(2,1)S(1)}, bf16[4,48,1536]{2,1,0:T(8,128)(2,1)S(1)}, u32[]{:S(2)}, u32[]{:S(2)}) collective-permute-start(bf16[4,48,1536]{2,1,0:T(8,128)(2,1)S(1)} %get-tuple-element.72), channel_id=1, source_target_pairs={{0,8},{8,0},{16,24},{24,16},{1,9},{9,1},{17,25},{25,17},{2,10},{10... | collective-permute-start | bytes 1769480 | tf_op jit(solution)/shard_map/ppermute | solution.py:38
  35.2 22.9 %collective-permute-start.6 = (bf16[4,48,1536]{2,1,0:T(8,128)(2,1)S(1)}, bf16[4,48,1536]{2,1,0:T(8,128)(2,1)S(1)}, u32[]{:S(2)}, u32[]{:S(2)}) collective-permute-start(bf16[4,48,1536]{2,1,0:T(8,128)(2,1)S(1)} %get-tuple-element.72), channel_id=1, source_target_pairs={{0,24},{8,16},{16,8},{24,0},{1,25},{9,17},{17,9},{25,1},{2,26},{10... | collective-permute-start | bytes 1769480 | tf_op jit(solution)/shard_map/ppermute | solution.py:38
  137.1 8.4 %collective-permute-start.9 = (bf16[416,1536]{1,0:T(8,128)(2,1)}, bf16[416,1536]{1,0:T(8,128)(2,1)}, u32[]{:S(2)}, u32[]{:S(2)}) collective-permute-start(bf16[416,1536]{1,0:T(8,128)(2,1)} %fusion.13), channel_id=1, source_target_pairs={{0,1},{1,0},{2,3},{3,2},{4,5},{5,4},{6,7},{7,6},{8,9},{9,8},{10,11... | collective-permute-start | bytes 3833864 | tf_op jit(solution)/shard_map/ppermute | solution.py:30
  148.1 20.4 %all-to-all-start.1 = ((bf16[4,104,1536]{2,1,0:T(8,128)(2,1)}), bf16[4,104,1536]{2,1,0:T(8,128)(2,1)S(1)}, u32[]{:S(2)}, u32[]{:S(2)}) async-start(bf16[4,104,1536]{2,1,0:T(8,128)(2,1)} %bitcast.212), calls=%async_computation.1 | async-start | bytes 2555904 | tf_op jit(solution)/shard_map/all_to_all | solution.py:200
  151.9 125.2 %reduce-scatter.2.cloned.1.call-start = ((), (), s32[]{:S(2)}) async-start(), calls=%async_computation.3 | async-start | bytes 5959680 | tf_op jit(solution)/shard_map/reduce_scatter | solution.py:195
  191.9 8.3 %collective-permute-start.11 = (bf16[197,768]{1,0:T(8,128)(2,1)S(1)}, bf16[197,768]{1,0:T(8,128)(2,1)S(1)}, u32[]{:S(2)}, u32[]{:S(2)}) collective-permute-start(bf16[197,768]{1,0:T(8,128)(2,1)S(1)} %fusion.46), channel_id=1, source_target_pairs={{0,1},{1,0},{2,3},{3,2},{4,5},{5,4},{6,7},{7,6},{8,9},{9,8},{10,11... | collective-permute-start | bytes 907784 | tf_op jit(solution)/shard_map/ppermute | solution.py:30
  196.6 44.8 %collective-permute-start.17 = (bf16[4,48,1536]{2,1,0:T(8,128)(2,1)}, bf16[4,48,1536]{2,1,0:T(8,128)(2,1)}, u32[]{:S(2)}, u32[]{:S(2)}) collective-permute-start(bf16[4,48,1536]{2,1,0:T(8,128)(2,1)} %get-tuple-element.75), channel_id=1, source_target_pairs={{0,8},{8,0},{16,24},{24,16},{1,9},{9,1},{17,25},{25,17},{2,10},{10... | collective-permute-start | bytes 1769480 | tf_op jit(solution)/shard_map/ppermute | solution.py:38
  198.1 43.4 %collective-permute-start.18 = (bf16[4,48,1536]{2,1,0:T(8,128)(2,1)}, bf16[4,48,1536]{2,1,0:T(8,128)(2,1)}, u32[]{:S(2)}, u32[]{:S(2)}) collective-permute-start(bf16[4,48,1536]{2,1,0:T(8,128)(2,1)} %get-tuple-element.76), channel_id=1, source_target_pairs={{0,16},{8,24},{16,0},{24,8},{1,17},{9,25},{17,1},{25,9},{2,18},{10... | collective-permute-start | bytes 1769480 | tf_op jit(solution)/shard_map/ppermute | solution.py:38
  198.6 42.8 %collective-permute-start.19 = (bf16[4,48,1536]{2,1,0:T(8,128)(2,1)S(1)}, bf16[4,48,1536]{2,1,0:T(8,128)(2,1)}, u32[]{:S(2)}, u32[]{:S(2)}) collective-permute-start(bf16[4,48,1536]{2,1,0:T(8,128)(2,1)S(1)} %get-tuple-element.77), channel_id=1, source_target_pairs={{0,24},{8,16},{16,8},{24,0},{1,25},{9,17},{17,9},{25,1},{2,26},{10... | collective-permute-start | bytes 1769480 | tf_op jit(solution)/shard_map/ppermute | solution.py:38
  203.4 22.8 %collective-permute-start.13 = (f32[11,768]{1,0:T(8,128)S(1)}, f32[11,768]{1,0:T(8,128)S(1)}, u32[]{:S(2)}, u32[]{:S(2)}) collective-permute-start(f32[11,768]{1,0:T(8,128)S(1)} %add.279), channel_id=1, source_target_pairs={{0,8},{8,0},{16,24},{24,16},{1,9},{9,1},{17,25},{25,17},{2,10},{10... | collective-permute-start | bytes 101384 | tf_op jit(solution)/shard_map/ppermute | solution.py:45
  230.4 8.2 %collective-permute-start.15 = (f32[11,768]{1,0:T(8,128)S(1)}, f32[11,768]{1,0:T(8,128)S(1)}, u32[]{:S(2)}, u32[]{:S(2)}) collective-permute-start(f32[11,768]{1,0:T(8,128)S(1)} %add.281), channel_id=1, source_target_pairs={{0,2},{2,0},{4,6},{6,4},{1,3},{3,1},{5,7},{7,5},{8,10},{10,8},{12,... | collective-permute-start | bytes 101384 | tf_op jit(solution)/shard_map/ppermute | solution.py:45
  238.6 12.4 %collective-permute-start.16 = (f32[11,768]{1,0:T(8,128)S(1)}, f32[11,768]{1,0:T(8,128)S(1)}, u32[]{:S(2)}, u32[]{:S(2)}) collective-permute-start(f32[11,768]{1,0:T(8,128)S(1)} %add.282), channel_id=1, source_target_pairs={{0,4},{2,6},{4,0},{6,2},{1,5},{3,7},{5,1},{7,3},{8,12},{10,14},{12... | collective-permute-start | bytes 101384 | tf_op jit(solution)/shard_map/ppermute | solution.py:45
  243.4 11.9 %collective-permute-start.20 = (bf16[48,1536]{1,0:T(8,128)(2,1)S(1)}, bf16[48,1536]{1,0:T(8,128)(2,1)S(1)}, u32[]{:S(2)}, u32[]{:S(2)}) collective-permute-start(bf16[48,1536]{1,0:T(8,128)(2,1)S(1)} %get-tuple-element.81), channel_id=1, source_target_pairs={{0,2},{2,4},{4,6},{6,0},{1,3},{3,5},{5,7},{7,1},{8,10},{10,12},{12... | collective-permute-start | bytes 442376 | tf_op jit(solution)/shard_map/ppermute | solution.py:51
  243.4 12.5 %collective-permute-start.22 = (bf16[48,1536]{1,0:T(8,128)(2,1)S(1)}, bf16[48,1536]{1,0:T(8,128)(2,1)S(1)}, u32[]{:S(2)}, u32[]{:S(2)}) collective-permute-start(bf16[48,1536]{1,0:T(8,128)(2,1)S(1)} %get-tuple-element.82), channel_id=1, source_target_pairs={{0,6},{2,0},{4,2},{6,4},{1,7},{3,1},{5,3},{7,5},{8,14},{10,8},{12,... | collective-permute-start | bytes 442376 | tf_op jit(solution)/shard_map/ppermute | solution.py:51
  247.2 16.0 %collective-permute-start.21 = (bf16[48,1536]{1,0:T(8,128)(2,1)S(1)}, bf16[48,1536]{1,0:T(8,128)(2,1)S(1)}, u32[]{:S(2)}, u32[]{:S(2)}) collective-permute-start(bf16[48,1536]{1,0:T(8,128)(2,1)S(1)} %get-tuple-element.83), channel_id=1, source_target_pairs={{0,4},{2,6},{4,0},{6,2},{1,5},{3,7},{5,1},{7,3},{8,12},{10,14},{12... | collective-permute-start | bytes 442376 | tf_op jit(solution)/shard_map/ppermute | solution.py:51
  266.8 8.4 %collective-permute-start.24 = (bf16[48,1536]{1,0:T(8,128)(2,1)S(1)}, bf16[48,1536]{1,0:T(8,128)(2,1)S(1)}, u32[]{:S(2)}, u32[]{:S(2)}) collective-permute-start(bf16[48,1536]{1,0:T(8,128)(2,1)S(1)} %get-tuple-element.65), channel_id=1, source_target_pairs={{0,16},{8,24},{16,0},{24,8},{1,17},{9,25},{17,1},{25,9},{2,18},{10... | collective-permute-start | bytes 442376 | tf_op jit(solution)/shard_map/ppermute | solution.py:38
  268.3 7.0 %collective-permute-start.25 = (bf16[48,1536]{1,0:T(8,128)(2,1)S(1)}, bf16[48,1536]{1,0:T(8,128)(2,1)S(1)}, u32[]{:S(2)}, u32[]{:S(2)}) collective-permute-start(bf16[48,1536]{1,0:T(8,128)(2,1)S(1)} %get-tuple-element.65), channel_id=1, source_target_pairs={{0,24},{8,16},{16,8},{24,0},{1,25},{9,17},{17,9},{25,1},{2,26},{10... | collective-permute-start | bytes 442376 | tf_op jit(solution)/shard_map/ppermute | solution.py:38
  (59 other events, 579.0 us)
Sparse Core Ops, SparseCore 0:
  9.7 58.9 all-gather.4
  70.2 51.5 all-gather.6
  159.3 96.3 reduce-scatter.1

commit v2 on v1

--- a/solution.py
+++ b/solution.py
@@ -225,6 +225,22 @@
     xhat_own, inverse_own = xhat1[0], inverse1[0]
     tokens_grad = grad_residual + norm_pull(xhat_own, inverse_own, norm1_gain, grad_normed)
 
+    bias_local = jnp.sum(grad_project, axis=(0, 1), dtype=F32)
+    bias_local = jnp.stack([bias_local[:local], bias_local[2 * local :]])
+    bias_full = lax.dynamic_update_slice_in_dim(
+        jnp.zeros((2, width), F32), bias_local, mp_index * local, 1
+    )
+    small = jnp.concatenate(
+        [
+            jnp.sum(grad_normed * xhat_own, axis=0)[None],
+            jnp.sum(grad_normed, axis=0)[None],
+            bias_full,
+            jnp.sum(grad_residual, axis=0)[None],
+            jnp.sum(grad_routed * xhat2, axis=0)[None],
+            jnp.sum(grad_routed, axis=0)[None],
+            router_grad.T,
+        ]
+    )
     attn_grad = jnp.concatenate([input_grad, output_grad], axis=1).astype(BF)
     attn_grad = attn_grad.reshape(dp_count, expert_axis, part, 4 * local)
     quarter = 0.0
@@ -232,6 +248,7 @@
         piece = lax.dynamic_index_in_dim(attn_grad, expert_index ^ j, 1, keepdims=False)
         quarter = quarter + (across(piece, j, expert_axis) if j else piece).astype(F32)
     quarter = quarter.astype(BF)
+    quarter, small = lax.optimization_barrier((quarter, small))
     share = 0.0
     for k in range(dp_count):
         piece = lax.dynamic_index_in_dim(
@@ -245,22 +262,6 @@
         attn_grad = lax.dynamic_update_slice(attn_grad, piece[None], (expert_index ^ j, 0, 0))
     attn_grad = attn_grad.reshape(-1, 4 * local)
 
-    bias_local = jnp.sum(grad_project, axis=(0, 1), dtype=F32)
-    bias_local = jnp.stack([bias_local[:local], bias_local[2 * local :]])
-    bias_full = lax.dynamic_update_slice_in_dim(
-        jnp.zeros((2, width), F32), bias_local, mp_index * local, 1
-    )
-    small = jnp.concatenate(
-        [
-            jnp.sum(grad_normed * xhat_own, axis=0)[None],
-            jnp.sum(grad_normed, axis=0)[None],
-            bias_full,
-            jnp.sum(grad_residual, axis=0)[None],
-            jnp.sum(grad_routed * xhat2, axis=0)[None],
-            jnp.sum(grad_routed, axis=0)[None],
-            router_grad.T,
-        ]
-    )
     small = sum_all(small)
     bias_total = expert_grad[2 * ff_part :][:1]
     return (

time: 291 us -> 292 us (level)
    ppermute x9, waiting for transfers between devices: 28 us -> 49.1 us  [across(): return lax.ppermute(value, 'expert', [(e, e ^ j) for e in range(count)])]
    ppermute x5, waiting for transfers between devices: 32.2 us -> 21.7 us  [sum_all(): lax.ppermute(value, axis, [(i, i ^ step) for i in range(count)])]
    ppermute x5, starting transfers between devices: 9.77 us -> 1.38 us  [sum_all(): lax.ppermute(value, axis, [(i, i ^ step) for i in range(count)])]
    ppermute x6, waiting for transfers between devices: 27 us -> 20.5 us  [to_owner(): lax.ppermute(chunk, 'dp', [(z, (z + k) % count) for z in range(count)])]
    ppermute x6, starting transfers between devices: 10 us -> 16.4 us  [to_owner(): lax.ppermute(chunk, 'dp', [(z, (z + k) % count) for z in range(count)])]
  transfers between devices with their start and end apart: 30 -> 30, of which waited for: 19 -> 17; matrix products, arithmetic and copies ran while one was open for 27% -> 27% of each run, Pallas kernels for 0% -> 0%
where the time goes in v2:
time: 292 us; the launch traced here: 290 us
  waiting for transfers between devices  118 us (40%)
  matrix products  56.3 us (19%)
  starting transfers between devices  32.5 us (11%)
  other arithmetic  24.5 us (8%)
  local copies, waits for them, and re-layouts  24.3 us (8%)
  blocking collectives  20.3 us (7%)
  between operations  14.9 us (5%)
    dot_general x26, matrix products, mm(): return jnp.einsum(spec, a, b, preferred_element_type=F32)  51.9 us
    ppermute x9, waiting for transfers between devices, across(): return lax.ppermute(value, 'expert', [(e, e ^ j) for e in range(count)])  49.1 us
    ppermute x5, waiting for transfers between devices, sum_all(): lax.ppermute(value, axis, [(i, i ^ step) for i in range(count)])  21.7 us
    ppermute x6, waiting for transfers between devices, to_owner(): lax.ppermute(chunk, 'dp', [(z, (z + k) % count) for z in range(count)])  20.5 us
    all_to_all x1, blocking collectives, on_device(): lax.all_to_all(send, 'expert', split_axis=0, concat_axis=0, tiled=True)  20.3 us
    ppermute x6, starting transfers between devices, to_owner(): lax.ppermute(chunk, 'dp', [(z, (z + k) % count) for z in range(count)])  16.4 us
    all_gather x1, waiting for transfers between devices, on_device(): down_full = lax.all_gather(down_weight[0], 'dp', axis=0, tiled=True)  14 us
    ppermute x9, starting transfers between devices, across(): return lax.ppermute(value, 'expert', [(e, e ^ j) for e in range(count)])  10.6 us
  transfers between devices with their start and end apart: 30, of which 17 were waited for; matrix products, arithmetic and copies ran while one was open for 27% of the time, Pallas kernels for 0%

profile of v2, /device:TPU:0, one launch (start us, length us, event | category | flops | bytes accessed | tf_op | source)
XLA Modules:
  0.0 290.5 jit_solution(769585263489042072)
XLA Ops:
  10.6 4.1 %collective-permute-start.2 = (bf16[56,1536]{1,0:T(8,128)(2,1)S(1)}, bf16[56,1536]{1,0:T(8,128)(2,1)S(1)}, u32[]{:S(2)}, u32[]{:S(2)}) collective-permute-start(bf16[56,1536]{1,0:T(8,128)(2,1)S(1)} %pad_maximum_fusion.7), channel_id=1, source_target_pairs={{0,4},{2,6},{4,0},{6,2},{1,5},{3,7},{5,1},{7,3},{8,12},{10,14},{12... | collective-permute-start | bytes 516104 | tf_op jit(solution)/shard_map/ppermute | solution.py:51
  17.0 8.6 %collective-permute-done.1 = bf16[56,1536]{1,0:T(8,128)(2,1)S(1)} collective-permute-done((bf16[56,1536]{1,0:T(8,128)(2,1)S(1)}, bf16[56,1536]{1,0:T(8,128)(2,1)S(1)}, u32[]{:S(2)}, u32[]{:S(2)}) %collective-permute-start.1) | collective-permute-done | bytes 172064 | tf_op jit(solution)/shard_map/ppermute | solution.py:51
  25.7 6.2 %collective-permute-done.3 = bf16[56,1536]{1,0:T(8,128)(2,1)S(1)} collective-permute-done((bf16[56,1536]{1,0:T(8,128)(2,1)S(1)}, bf16[56,1536]{1,0:T(8,128)(2,1)S(1)}, u32[]{:S(2)}, u32[]{:S(2)}) %collective-permute-start.3) | collective-permute-done | bytes 172064 | tf_op jit(solution)/shard_map/ppermute | solution.py:51
  36.4 13.6 %collective-permute-done.4 = bf16[4,48,1536]{2,1,0:T(8,128)(2,1)S(1)} collective-permute-done((bf16[4,48,1536]{2,1,0:T(8,128)(2,1)S(1)}, bf16[4,48,1536]{2,1,0:T(8,128)(2,1)S(1)}, u32[]{:S(2)}, u32[]{:S(2)}) %collective-permute-start.4) | collective-permute-done | bytes 589856 | tf_op jit(solution)/shard_map/ppermute | solution.py:38
  50.1 8.0 %collective-permute-done.6 = bf16[4,48,1536]{2,1,0:T(8,128)(2,1)S(1)} collective-permute-done((bf16[4,48,1536]{2,1,0:T(8,128)(2,1)S(1)}, bf16[4,48,1536]{2,1,0:T(8,128)(2,1)S(1)}, u32[]{:S(2)}, u32[]{:S(2)}) %collective-permute-start.6) | collective-permute-done | bytes 589856 | tf_op jit(solution)/shard_map/ppermute | solution.py:38
  66.0 3.5 %fusion.120 = (f32[2,6,197]{2,1,0:T(8,128)S(1)}, f32[2,6,197,197]{2,3,1,0:T(8,128)}) fusion(bf16[2,197,6,64]{1,3,2,0:T(8,128)(2,1)S(1)} %bitcast.232, bf16[2,197,6,64]{1,3,2,0:T(8,128)(2,1)} %bitcast.234), kind=kOutput, calls=%fused_computation.238 | convolution fusion | flops 61007944 | bytes 2477472 | tf_op jit(solution)/shard_map/sub | solution.py:62
  77.1 20.3 %all_to_all.10 = bf16[4,104,1536]{2,1,0:T(8,128)(2,1)S(1)} all-to-all(bf16[4,104,1536]{2,1,0:T(8,128)(2,1)S(1)} %bitcast.205), channel_id=1, replica_groups=mesh['expert'=4,'dp'=4,'mp'=2] {'expert'}, dimensions={0} | all-to-all | bytes 2555904 | tf_op jit(solution)/shard_map/all_to_all | solution.py:165
  100.4 7.4 %multiply_convert_fusion = (bf16[832,1536]{1,0:T(8,128)(2,1)}, f32[832,1536]{1,0:T(8,128)}) fusion(f32[1536]{0:T(1024)S(1)} %reshape.230, bf16[1,768,1536]{2,1,0:T(8,128)(2,1)} %all-gather.5.cloned.1.call-done, bf16[416,1536]{1,0:T(8,128)(2,1)S(1)} %bitcast.207, bf16[416,1536]{1,0:T(8,128)(2,1)S(1)} %collective-permute-done.8), kind=kOutput, calls=%fused_computation.12 | convolution fusion | flops 1973157888 | bytes 12589056 | tf_op jit(solution)/shard_map/td,df->tf/dot_general | solution.py:13
  107.8 14.0 %all-gather.7.cloned.1.call-done = bf16[1,1536,768]{2,1,0:T(8,128)(2,1)} async-done(((bf16[1,384,768]{2,1,0:T(8,128)(2,1)}), bf16[1,1536,768]{2,1,0:T(8,128)(2,1)}) %all-gather.7.cloned.1.call-update) | async-done | bytes 2359312 | tf_op jit(solution)/shard_map/all_gather | solution.py:117
  121.8 7.7 %fusion.123 = (bf16[1536]{0:T(1024)(128)(2,1)}, bf16[832,1536]{1,0:T(8,128)(2,1)S(1)}) fusion(f32[832,1536]{1,0:T(8,128)} %get-tuple-element.105, f32[1536]{0:T(1024)S(1)} %reshape.230, bf16[1,1536,768]{2,1,0:T(8,128)(2,1)} %all-gather.7.cloned.1.call-done, bf16[416,1536]{1,0:T(8,128)(2,1)S(1)} %collective-permute-done.8, bf16[416,1536]{1,0:T(8,128)(2,1)S(1)} %bitcast.208), kind=kOutput, calls=%fused_computation.241 | convolution fusion | flops 1980824064 | bytes 12592128 | tf_op jit(solution)/shard_map/td,fd->tf/dot_general | solution.py:13
  140.9 6.3 %convolution_convert_fusion.1 = bf16[1536,768]{1,0:T(8,128)(2,1)} fusion(bf16[832,1536]{1,0:T(8,128)(2,1)} %get-tuple-element.104, bf16[416,1536]{1,0:T(8,128)(2,1)} %copy-done.23, bf16[416,1536]{1,0:T(8,128)(2,1)} %bitcast.209), kind=kOutput, calls=%fused_computation.22 | convolution fusion | flops 1966669824 | bytes 7471104 | tf_op jit(solution)/shard_map/tf,td->fd/dot_general | solution.py:13
  147.2 2.7 fusion.12
  149.9 3.8 %all-to-all-start.1 = ((bf16[4,104,1536]{2,1,0:T(8,128)(2,1)}), bf16[4,104,1536]{2,1,0:T(8,128)(2,1)S(1)}, u32[]{:S(2)}, u32[]{:S(2)}) async-start(bf16[4,104,1536]{2,1,0:T(8,128)(2,1)} %bitcast.212), calls=%async_computation.1 | async-start | bytes 2555904 | tf_op jit(solution)/shard_map/all_to_all | solution.py:200
  153.7 4.7 %convolution_convert_fusion = bf16[1536,768]{1,0:T(8,128)(2,1)S(1)} fusion(bf16[832,1536]{1,0:T(8,128)(2,1)} %copy-done.47, bf16[416,1536]{1,0:T(8,128)(2,1)S(1)} %bitcast.211, bf16[416,1536]{1,0:T(8,128)(2,1)} %copy-done.23), kind=kOutput, calls=%fused_computation.21 | convolution fusion | flops 1966669824 | bytes 7471104 | tf_op jit(solution)/shard_map/tf,td->fd/dot_general | solution.py:13
  158.4 2.5 fusion.8
  160.9 9.6 %all-to-all-done.1 = bf16[4,104,1536]{2,1,0:T(8,128)(2,1)S(1)} async-done(((bf16[4,104,1536]{2,1,0:T(8,128)(2,1)}), bf16[4,104,1536]{2,1,0:T(8,128)(2,1)S(1)}, u32[]{:S(2)}, u32[]{:S(2)}) %all-to-all-start.1) | async-done | bytes 1277984 | tf_op jit(solution)/shard_map/all_to_all | solution.py:200
  180.7 2.4 multiply_reduce_fusion
  200.4 11.0 %collective-permute-done.12 = bf16[4,48,1536]{2,1,0:T(8,128)(2,1)} collective-permute-done((bf16[4,48,1536]{2,1,0:T(8,128)(2,1)}, bf16[4,48,1536]{2,1,0:T(8,128)(2,1)}, u32[]{:S(2)}, u32[]{:S(2)}) %collective-permute-start.12) | collective-permute-done | bytes 589856 | tf_op jit(solution)/shard_map/ppermute | solution.py:38
  211.5 13.3 %collective-permute-done.13 = bf16[4,48,1536]{2,1,0:T(8,128)(2,1)} collective-permute-done((bf16[4,48,1536]{2,1,0:T(8,128)(2,1)}, bf16[4,48,1536]{2,1,0:T(8,128)(2,1)}, u32[]{:S(2)}, u32[]{:S(2)}) %collective-permute-start.13) | collective-permute-done | bytes 589856 | tf_op jit(solution)/shard_map/ppermute | solution.py:38
  228.5 3.5 %collective-permute-done.16 = f32[11,768]{1,0:T(8,128)S(1)} collective-permute-done((f32[11,768]{1,0:T(8,128)S(1)}, f32[11,768]{1,0:T(8,128)S(1)}, u32[]{:S(2)}, u32[]{:S(2)}) %collective-permute-start.16) | collective-permute-done | bytes 33824 | tf_op jit(solution)/shard_map/ppermute | solution.py:45
  232.6 6.3 %collective-permute-start.20 = (bf16[48,1536]{1,0:T(8,128)(2,1)S(1)}, bf16[48,1536]{1,0:T(8,128)(2,1)S(1)}, u32[]{:S(2)}, u32[]{:S(2)}) collective-permute-start(bf16[48,1536]{1,0:T(8,128)(2,1)S(1)} %get-tuple-element.85), channel_id=1, source_target_pairs={{0,2},{2,4},{4,6},{6,0},{1,3},{3,5},{5,7},{7,1},{8,10},{10,12},{12... | collective-permute-start | bytes 442376 | tf_op jit(solution)/shard_map/ppermute | solution.py:51
  238.9 3.9 %collective-permute-start.21 = (bf16[48,1536]{1,0:T(8,128)(2,1)S(1)}, bf16[48,1536]{1,0:T(8,128)(2,1)S(1)}, u32[]{:S(2)}, u32[]{:S(2)}) collective-permute-start(bf16[48,1536]{1,0:T(8,128)(2,1)S(1)} %get-tuple-element.87), channel_id=1, source_target_pairs={{0,4},{2,6},{4,0},{6,2},{1,5},{3,7},{5,1},{7,3},{8,12},{10,14},{12... | collective-permute-start | bytes 442376 | tf_op jit(solution)/shard_map/ppermute | solution.py:51
  244.0 17.0 %collective-permute-done.18 = f32[11,768]{1,0:T(8,128)S(1)} collective-permute-done((f32[11,768]{1,0:T(8,128)S(1)}, f32[11,768]{1,0:T(8,128)S(1)}, u32[]{:S(2)}, u32[]{:S(2)}) %collective-permute-start.18) | collective-permute-done | bytes 33824 | tf_op jit(solution)/shard_map/ppermute | solution.py:45
  261.1 5.8 %collective-permute-done.21 = bf16[48,1536]{1,0:T(8,128)(2,1)S(1)} collective-permute-done((bf16[48,1536]{1,0:T(8,128)(2,1)S(1)}, bf16[48,1536]{1,0:T(8,128)(2,1)S(1)}, u32[]{:S(2)}, u32[]{:S(2)}) %collective-permute-start.21) | collective-permute-done | bytes 147488 | tf_op jit(solution)/shard_map/ppermute | solution.py:51
  (278 shorter events, 89.4 us)
Async XLA Ops:
  7.2 92.6 %all-gather.5.cloned.1.call-start = ((), (), s32[]{:S(2)}) async-start(), calls=%async_computation.4 | async-start | bytes 2949120 | tf_op jit(solution)/shard_map/all_gather | solution.py:116
  8.0 113.9 %all-gather.7.cloned.1.call-start = ((), (), s32[]{:S(2)}) async-start(), calls=%async_computation.5 | async-start | bytes 2949120 | tf_op jit(solution)/shard_map/all_gather | solution.py:117
  10.6 15.0 %collective-permute-start.2 = (bf16[56,1536]{1,0:T(8,128)(2,1)S(1)}, bf16[56,1536]{1,0:T(8,128)(2,1)S(1)}, u32[]{:S(2)}, u32[]{:S(2)}) collective-permute-start(bf16[56,1536]{1,0:T(8,128)(2,1)S(1)} %pad_maximum_fusion.7), channel_id=1, source_target_pairs={{0,4},{2,6},{4,0},{6,2},{1,5},{3,7},{5,1},{7,3},{8,12},{10,14},{12... | collective-permute-start | bytes 516104 | tf_op jit(solution)/shard_map/ppermute | solution.py:51
  14.7 10.9 %collective-permute-start.1 = (bf16[56,1536]{1,0:T(8,128)(2,1)S(1)}, bf16[56,1536]{1,0:T(8,128)(2,1)S(1)}, u32[]{:S(2)}, u32[]{:S(2)}) collective-permute-start(bf16[56,1536]{1,0:T(8,128)(2,1)S(1)} %pad_maximum_fusion.7), channel_id=1, source_target_pairs={{0,6},{2,0},{4,2},{6,4},{1,7},{3,1},{5,3},{7,5},{8,14},{10,8},{12,... | collective-permute-start | bytes 516104 | tf_op jit(solution)/shard_map/ppermute | solution.py:51
  16.1 15.8 %collective-permute-start.3 = (bf16[56,1536]{1,0:T(8,128)(2,1)S(1)}, bf16[56,1536]{1,0:T(8,128)(2,1)S(1)}, u32[]{:S(2)}, u32[]{:S(2)}) collective-permute-start(bf16[56,1536]{1,0:T(8,128)(2,1)S(1)} %pad_maximum_fusion.7), channel_id=1, source_target_pairs={{0,2},{2,4},{4,6},{6,0},{1,3},{3,5},{5,7},{7,1},{8,10},{10,12},{12... | collective-permute-start | bytes 516104 | tf_op jit(solution)/shard_map/ppermute | solution.py:51
  16.7 19.1 %collective-permute-start = (bf16[197,768]{1,0:T(8,128)(2,1)S(1)}, bf16[197,768]{1,0:T(8,128)(2,1)S(1)}, u32[]{:S(2)}, u32[]{:S(2)}) collective-permute-start(bf16[197,768]{1,0:T(8,128)(2,1)S(1)} %copy-done.8), channel_id=1, source_target_pairs={{0,1},{1,0},{2,3},{3,2},{4,5},{5,4},{6,7},{7,6},{8,9},{9,8},{10,11... | collective-permute-start | bytes 907784 | tf_op jit(solution)/shard_map/ppermute | solution.py:30
  32.3 17.7 %collective-permute-start.5 = (bf16[4,48,1536]{2,1,0:T(8,128)(2,1)S(1)}, bf16[4,48,1536]{2,1,0:T(8,128)(2,1)S(1)}, u32[]{:S(2)}, u32[]{:S(2)}) collective-permute-start(bf16[4,48,1536]{2,1,0:T(8,128)(2,1)S(1)} %get-tuple-element.76), channel_id=1, source_target_pairs={{0,16},{8,24},{16,0},{24,8},{1,17},{9,25},{17,1},{25,9},{2,18},{10... | collective-permute-start | bytes 1769480 | tf_op jit(solution)/shard_map/ppermute | solution.py:38
  33.7 16.3 %collective-permute-start.4 = (bf16[4,48,1536]{2,1,0:T(8,128)(2,1)S(1)}, bf16[4,48,1536]{2,1,0:T(8,128)(2,1)S(1)}, u32[]{:S(2)}, u32[]{:S(2)}) collective-permute-start(bf16[4,48,1536]{2,1,0:T(8,128)(2,1)S(1)} %get-tuple-element.76), channel_id=1, source_target_pairs={{0,8},{8,0},{16,24},{24,16},{1,9},{9,1},{17,25},{25,17},{2,10},{10... | collective-permute-start | bytes 1769480 | tf_op jit(solution)/shard_map/ppermute | solution.py:38
  35.2 22.9 %collective-permute-start.6 = (bf16[4,48,1536]{2,1,0:T(8,128)(2,1)S(1)}, bf16[4,48,1536]{2,1,0:T(8,128)(2,1)S(1)}, u32[]{:S(2)}, u32[]{:S(2)}) collective-permute-start(bf16[4,48,1536]{2,1,0:T(8,128)(2,1)S(1)} %get-tuple-element.76), channel_id=1, source_target_pairs={{0,24},{8,16},{16,8},{24,0},{1,25},{9,17},{17,9},{25,1},{2,26},{10... | collective-permute-start | bytes 1769480 | tf_op jit(solution)/shard_map/ppermute | solution.py:38
  137.0 10.2 %collective-permute-start.9 = (bf16[416,1536]{1,0:T(8,128)(2,1)}, bf16[416,1536]{1,0:T(8,128)(2,1)}, u32[]{:S(2)}, u32[]{:S(2)}) collective-permute-start(bf16[416,1536]{1,0:T(8,128)(2,1)} %fusion.13), channel_id=1, source_target_pairs={{0,1},{1,0},{2,3},{3,2},{4,5},{5,4},{6,7},{7,6},{8,9},{9,8},{10,11... | collective-permute-start | bytes 3833864 | tf_op jit(solution)/shard_map/ppermute | solution.py:30
  149.9 20.7 %all-to-all-start.1 = ((bf16[4,104,1536]{2,1,0:T(8,128)(2,1)}), bf16[4,104,1536]{2,1,0:T(8,128)(2,1)S(1)}, u32[]{:S(2)}, u32[]{:S(2)}) async-start(bf16[4,104,1536]{2,1,0:T(8,128)(2,1)} %bitcast.212), calls=%async_computation.1 | async-start | bytes 2555904 | tf_op jit(solution)/shard_map/all_to_all | solution.py:200
  153.7 123.9 %reduce-scatter.2.cloned.1.call-start = ((), (), s32[]{:S(2)}) async-start(), calls=%async_computation.3 | async-start | bytes 5959680 | tf_op jit(solution)/shard_map/reduce_scatter | solution.py:195
  191.6 7.0 %collective-permute-start.11 = (bf16[197,768]{1,0:T(8,128)(2,1)S(1)}, bf16[197,768]{1,0:T(8,128)(2,1)S(1)}, u32[]{:S(2)}, u32[]{:S(2)}) collective-permute-start(bf16[197,768]{1,0:T(8,128)(2,1)S(1)} %fusion.46), channel_id=1, source_target_pairs={{0,1},{1,0},{2,3},{3,2},{4,5},{5,4},{6,7},{7,6},{8,9},{9,8},{10,11... | collective-permute-start | bytes 907784 | tf_op jit(solution)/shard_map/ppermute | solution.py:30
  195.0 16.4 %collective-permute-start.12 = (bf16[4,48,1536]{2,1,0:T(8,128)(2,1)}, bf16[4,48,1536]{2,1,0:T(8,128)(2,1)}, u32[]{:S(2)}, u32[]{:S(2)}) collective-permute-start(bf16[4,48,1536]{2,1,0:T(8,128)(2,1)} %get-tuple-element.79), channel_id=1, source_target_pairs={{0,8},{8,0},{16,24},{24,16},{1,9},{9,1},{17,25},{25,17},{2,10},{10... | collective-permute-start | bytes 1769480 | tf_op jit(solution)/shard_map/ppermute | solution.py:38
  196.4 28.3 %collective-permute-start.13 = (bf16[4,48,1536]{2,1,0:T(8,128)(2,1)}, bf16[4,48,1536]{2,1,0:T(8,128)(2,1)}, u32[]{:S(2)}, u32[]{:S(2)}) collective-permute-start(bf16[4,48,1536]{2,1,0:T(8,128)(2,1)} %get-tuple-element.80), channel_id=1, source_target_pairs={{0,16},{8,24},{16,0},{24,8},{1,17},{9,25},{17,1},{25,9},{2,18},{10... | collective-permute-start | bytes 1769480 | tf_op jit(solution)/shard_map/ppermute | solution.py:38
  197.1 27.6 %collective-permute-start.14 = (bf16[4,48,1536]{2,1,0:T(8,128)(2,1)}, bf16[4,48,1536]{2,1,0:T(8,128)(2,1)}, u32[]{:S(2)}, u32[]{:S(2)}) collective-permute-start(bf16[4,48,1536]{2,1,0:T(8,128)(2,1)} %get-tuple-element.81), channel_id=1, source_target_pairs={{0,24},{8,16},{16,8},{24,0},{1,25},{9,17},{17,9},{25,1},{2,26},{10... | collective-permute-start | bytes 1769480 | tf_op jit(solution)/shard_map/ppermute | solution.py:38
  232.0 10.8 %collective-permute-start.17 = (f32[11,768]{1,0:T(8,128)S(1)}, f32[11,768]{1,0:T(8,128)S(1)}, u32[]{:S(2)}, u32[]{:S(2)}) collective-permute-start(f32[11,768]{1,0:T(8,128)S(1)} %add.283), channel_id=1, source_target_pairs={{0,16},{8,24},{16,0},{24,8},{1,17},{9,25},{17,1},{25,9},{2,18},{10... | collective-permute-start | bytes 101384 | tf_op jit(solution)/shard_map/ppermute | solution.py:45
  232.6 28.4 %collective-permute-start.20 = (bf16[48,1536]{1,0:T(8,128)(2,1)S(1)}, bf16[48,1536]{1,0:T(8,128)(2,1)S(1)}, u32[]{:S(2)}, u32[]{:S(2)}) collective-permute-start(bf16[48,1536]{1,0:T(8,128)(2,1)S(1)} %get-tuple-element.85), channel_id=1, source_target_pairs={{0,2},{2,4},{4,6},{6,0},{1,3},{3,5},{5,7},{7,1},{8,10},{10,12},{12... | collective-permute-start | bytes 442376 | tf_op jit(solution)/shard_map/ppermute | solution.py:51
  238.9 22.1 %collective-permute-start.22 = (bf16[48,1536]{1,0:T(8,128)(2,1)S(1)}, bf16[48,1536]{1,0:T(8,128)(2,1)S(1)}, u32[]{:S(2)}, u32[]{:S(2)}) collective-permute-start(bf16[48,1536]{1,0:T(8,128)(2,1)S(1)} %get-tuple-element.86), channel_id=1, source_target_pairs={{0,6},{2,0},{4,2},{6,4},{1,7},{3,1},{5,3},{7,5},{8,14},{10,8},{12,... | collective-permute-start | bytes 442376 | tf_op jit(solution)/shard_map/ppermute | solution.py:51
  238.9 27.9 %collective-permute-start.21 = (bf16[48,1536]{1,0:T(8,128)(2,1)S(1)}, bf16[48,1536]{1,0:T(8,128)(2,1)S(1)}, u32[]{:S(2)}, u32[]{:S(2)}) collective-permute-start(bf16[48,1536]{1,0:T(8,128)(2,1)S(1)} %get-tuple-element.87), channel_id=1, source_target_pairs={{0,4},{2,6},{4,0},{6,2},{1,5},{3,7},{5,1},{7,3},{8,12},{10,14},{12... | collective-permute-start | bytes 442376 | tf_op jit(solution)/shard_map/ppermute | solution.py:51
  242.9 18.1 %collective-permute-start.18 = (f32[11,768]{1,0:T(8,128)S(1)}, f32[11,768]{1,0:T(8,128)S(1)}, u32[]{:S(2)}, u32[]{:S(2)}) collective-permute-start(f32[11,768]{1,0:T(8,128)S(1)} %add.284), channel_id=1, source_target_pairs={{0,2},{2,0},{4,6},{6,4},{1,3},{3,1},{5,7},{7,5},{8,10},{10,8},{12,... | collective-permute-start | bytes 101384 | tf_op jit(solution)/shard_map/ppermute | solution.py:45
  261.0 9.6 %collective-permute-start.19 = (f32[11,768]{1,0:T(8,128)S(1)}, f32[11,768]{1,0:T(8,128)S(1)}, u32[]{:S(2)}, u32[]{:S(2)}) collective-permute-start(f32[11,768]{1,0:T(8,128)S(1)} %add.285), channel_id=1, source_target_pairs={{0,4},{2,6},{4,0},{6,2},{1,5},{3,7},{5,1},{7,3},{8,12},{10,14},{12... | collective-permute-start | bytes 101384 | tf_op jit(solution)/shard_map/ppermute | solution.py:45
  267.0 6.7 %collective-permute-start.24 = (bf16[48,1536]{1,0:T(8,128)(2,1)S(1)}, bf16[48,1536]{1,0:T(8,128)(2,1)S(1)}, u32[]{:S(2)}, u32[]{:S(2)}) collective-permute-start(bf16[48,1536]{1,0:T(8,128)(2,1)S(1)} %get-tuple-element.69), channel_id=1, source_target_pairs={{0,16},{8,24},{16,0},{24,8},{1,17},{9,25},{17,1},{25,9},{2,18},{10... | collective-permute-start | bytes 442376 | tf_op jit(solution)/shard_map/ppermute | solution.py:38
  269.7 6.0 %collective-permute-start.25 = (bf16[48,1536]{1,0:T(8,128)(2,1)S(1)}, bf16[48,1536]{1,0:T(8,128)(2,1)S(1)}, u32[]{:S(2)}, u32[]{:S(2)}) collective-permute-start(bf16[48,1536]{1,0:T(8,128)(2,1)S(1)} %get-tuple-element.69), channel_id=1, source_target_pairs={{0,24},{8,16},{16,8},{24,0},{1,25},{9,17},{17,9},{25,1},{2,26},{10... | collective-permute-start | bytes 442376 | tf_op jit(solution)/shard_map/ppermute | solution.py:38
  (56 other events, 666.3 us)
Sparse Core Ops, SparseCore 0:
  9.7 58.9 all-gather.4
  70.2 51.5 all-gather.6
  161.0 102.4 reduce-scatter.1
